TPU v7x, 128 devices: a whole 4x4x4 slice. The times are simulated.
128 devices in a mesh: seq: 32 (over z, y_lo, x), rep: 4 (over y_hi, core).
Axes of the slice: x: 4, y: 4 (y_hi: 2, y_lo: 2; y = y_hi * 2 + y_lo), z: 4, core: 2. Of those that a mesh axis runs over, the one named last changes fastest.
Arguments:
- queries: bfloat16 [4, 32768, 768], P('rep', 'seq'), may hold values from -6 to 6
- key_rows: bfloat16 [4, 32768, 768], P('rep', 'seq'), may hold values from -6 to 6
- value_rows: bfloat16 [4, 32768, 768], P('rep', 'seq'), may hold values from -6 to 6
- saved_out: bfloat16 [4, 32768, 768], P('rep', 'seq'), may hold values from -12 to 12
- logsumexp: float32 [4, 12, 32768], P('rep', None, 'seq'), may hold values from 7 to 8
- out_grad: bfloat16 [4, 32768, 768], P('rep', 'seq'), may hold values from -3 to 3
- proj_weight: bfloat16 [768, 768], replicated, may hold values from -0.21875 to 0.21875
Outputs:
- grad_query: bfloat16 [4, 32768, 768], P('rep', 'seq')
- grad_key: bfloat16 [4, 32768, 768], P('rep', 'seq')
- grad_value: bfloat16 [4, 32768, 768], P('rep', 'seq')
- projection_gradient: float32 [768, 768], P('seq')
All inputs are finite; a program needn't handle non-finite values.
Results may differ from a plain program's by a relative error of at most 0.0057.
Values may be sent and summed in bfloat16 or wider, within the bound.
No kernel may reach another device: no remote copies, remote signals or barrier semaphores. Data moves between devices by JAX's collectives and lax.ppermute only.
A program may use at most 128 MiB of HBM per device.

v0:
```python
import math

import jax
import jax.numpy as jnp
from jax import lax
from jax.sharding import PartitionSpec as P

DILATION_STEP = 128


def on_device(queries, key_rows, value_rows, saved_out, logsumexp, out_grad, proj_weight):
    query_mat = queries[0]
    key_mat = key_rows[0]
    value_mat = value_rows[0]
    saved_mat = saved_out[0]
    grad_mat = out_grad[0]
    logsum_matrix = logsumexp[0]
    token_count, width = query_mat.shape
    head_number = logsum_matrix.shape[0]
    head_width = width // head_number
    scaling = head_width ** (-0.5)
    dilated_rows = token_count // DILATION_STEP
    seq_count = lax.axis_size("seq")
    rep_count = lax.axis_size("rep")
    attn_grad = lax.dot_general(
        grad_mat, proj_weight, (((1,), (1,)), ((), ())), preferred_element_type=jnp.float32
    ).astype(jnp.bfloat16)
    shard_sum = lax.psum_scatter(
        lax.dot_general(
            saved_mat, grad_mat, (((0,), (0,)), ((), ())), preferred_element_type=jnp.float32
        ),
        "seq",
        scatter_dimension=0,
        tiled=True,
    )
    weight_sum = lax.psum(shard_sum, "rep")
    projection_gradient = weight_sum * (1.0 / math.sqrt(rep_count * seq_count * token_count))
    shape3 = (token_count, head_number, head_width)
    query_tensor = query_mat.reshape(shape3)
    key_tensor = key_mat.reshape(shape3)
    value_tensor = value_mat.reshape(shape3)
    attention_output = attn_grad.reshape(shape3)
    saved3 = saved_mat.reshape(shape3)
    delta_value = jnp.sum(attention_output.astype(jnp.float32) * saved3.astype(jnp.float32), axis=2)

    def one_head(inputs):
        head_query, head_key, head_value, head_grad, head_lse, head_delta = inputs
        score_matrix = (
            lax.dot_general(
                head_query, head_key, (((1,), (1,)), ((), ())), preferred_element_type=jnp.float32
            )
            * scaling
        )
        probability = jnp.exp(score_matrix - head_lse[:, None])
        probs_gradient = lax.dot_general(
            head_grad, head_value, (((1,), (1,)), ((), ())), preferred_element_type=jnp.float32
        )
        scores_gradient = (probability * (probs_gradient - head_delta[:, None])).astype(
            jnp.bfloat16
        )
        weight_matrix = probability.astype(jnp.bfloat16)
        query_gradient = (
            jnp.dot(scores_gradient, head_key, preferred_element_type=jnp.float32) * scaling
        )
        grad_k = (
            lax.dot_general(
                scores_gradient,
                head_query,
                (((0,), (0,)), ((), ())),
                preferred_element_type=jnp.float32,
            )
            * scaling
        )
        value_gradient = lax.dot_general(
            weight_matrix, head_grad, (((0,), (0,)), ((), ())), preferred_element_type=jnp.float32
        )
        return (query_gradient, grad_k, value_gradient)

    def heads_leading(array_input):
        return jnp.transpose(array_input, (1, 0, 2))

    local_query, local_key, local_value = lax.map(
        one_head,
        (
            heads_leading(query_tensor),
            heads_leading(key_tensor),
            heads_leading(value_tensor),
            heads_leading(attention_output),
            logsum_matrix,
            delta_value.T,
        ),
    )
    index_rows = jnp.arange(head_number)

    def pick_rows(array_input):
        return array_input.reshape(dilated_rows, DILATION_STEP, head_number, head_width)[
            :, index_rows, index_rows
        ]

    dilated_query = pick_rows(query_tensor)
    dilated_key = pick_rows(key_tensor)
    dilated_value = pick_rows(value_tensor)
    dilated_gradient = pick_rows(attention_output)
    dilated_logsum = logsum_matrix.reshape(head_number, dilated_rows, DILATION_STEP)[
        index_rows, :, index_rows
    ]
    dilated_delta = delta_value.reshape(dilated_rows, DILATION_STEP, head_number)[
        :, index_rows, index_rows
    ]

    def join_heads(array_input):
        return array_input.reshape(array_input.shape[0], width)

    def divide_heads(array_input):
        return array_input.reshape(array_input.shape[0], head_number, head_width)

    segment_key = divide_heads(lax.all_gather(join_heads(dilated_key), "seq", axis=0, tiled=True))
    segment_value = divide_heads(
        lax.all_gather(join_heads(dilated_value), "seq", axis=0, tiled=True)
    )
    score_matrix = (
        jnp.einsum("iwq,rwq->wir", dilated_query, segment_key, preferred_element_type=jnp.float32)
        * scaling
    )
    probability = jnp.exp(score_matrix - dilated_logsum[:, :, None])
    probs_gradient = jnp.einsum(
        "iwq,rwq->wir", dilated_gradient, segment_value, preferred_element_type=jnp.float32
    )
    scores_gradient = (probability * (probs_gradient - dilated_delta.T[:, :, None])).astype(
        jnp.bfloat16
    )
    scores_gradient, weight_matrix = (scores_gradient, probability.astype(jnp.bfloat16))
    query_gradient = scaling * jnp.einsum(
        "tvq,qta->vta", scores_gradient, segment_key, preferred_element_type=jnp.float32
    )
    grad_k = scaling * jnp.einsum(
        "gws,wgt->sgt", scores_gradient, dilated_query, preferred_element_type=jnp.float32
    )
    value_gradient = jnp.einsum(
        "gws,wgt->sgt", weight_matrix, dilated_gradient, preferred_element_type=jnp.float32
    )
    key_total, value_total = (
        lax.psum_scatter(join_heads(grad_k), "seq", scatter_dimension=0, tiled=True),
        lax.psum_scatter(join_heads(value_gradient), "seq", scatter_dimension=0, tiled=True),
    )
    dilated_key_grad = divide_heads(key_total)
    dilated_value_grad = divide_heads(value_total)

    def place_rows(array_input):
        full_sequence = (
            jnp.zeros((dilated_rows, DILATION_STEP, head_number, head_width), jnp.float32)
            .at[:, index_rows, index_rows]
            .set(array_input)
        )
        return full_sequence.reshape(shape3)

    def finish_heads(local_piece, dilated_piece):
        total_sum = heads_leading(local_piece) + place_rows(dilated_piece)
        return total_sum.astype(jnp.bfloat16).reshape(token_count, width)[None]

    return (
        finish_heads(local_query, query_gradient),
        finish_heads(local_key, dilated_key_grad),
        finish_heads(local_value, dilated_value_grad),
        projection_gradient,
    )


def solution(mesh):
    in_specs = (
        P("rep", "seq", None),
        P("rep", "seq", None),
        P("rep", "seq", None),
        P("rep", "seq", None),
        P("rep", None, "seq"),
        P("rep", "seq", None),
        P(),
    )
    out_specs = (
        P("rep", "seq", None),
        P("rep", "seq", None),
        P("rep", "seq", None),
        P("seq", None),
    )
    return jax.shard_map(
        on_device, mesh=mesh, in_specs=in_specs, out_specs=out_specs, check_vma=False
    )
```

profile of v0, /device:TPU:2, one launch (start us, length us, event | category | flops | bytes accessed | tf_op | source)
XLA Modules:
  0.0 673.9 jit_solution(14635360464637519059)
XLA Ops:
  13.6 3.0 copy.81
  16.6 7.1 %copy.54 = bf16[8,128,12,64]{3,0,2,1:T(8,128)(2,1)} copy(bf16[8,128,12,64]{1,0,3,2:T(8,128)(2,1)} %bitcast.201) | data formatting | bytes 3145728 | tf_op jit(solution)/shard_map/reshape;reshape;squeeze | solution.py:96
  26.4 84.5 %all_gather.6 = bf16[256,768]{1,0:T(8,128)(2,1)} all-gather(bf16[8,768]{1,0:T(8,128)(2,1)S(1)} %reshape.56), channel_id=1, replica_groups=mesh['seq'=32,'rep'=4] {'seq'}, dimensions={0}, use_global_device_ids=true | all-gather | bytes 405504 | tf_op jit(solution)/shard_map/all_gather | solution.py:117
  113.7 7.1 %copy.58 = bf16[8,128,12,64]{3,0,2,1:T(8,128)(2,1)} copy(bf16[8,128,12,64]{1,0,3,2:T(8,128)(2,1)} %bitcast.202) | data formatting | bytes 3145728 | tf_op jit(solution)/shard_map/reshape;reshape;squeeze | solution.py:96
  120.8 3.1 gather_fusion.1
  129.3 7.1 %copy.60 = bf16[8,128,12,64]{3,0,2,1:T(8,128)(2,1)} copy(bf16[8,128,12,64]{1,0,3,2:T(8,128)(2,1)} %bitcast.203) | data formatting | bytes 3145728 | tf_op jit(solution)/shard_map/reshape;reshape | solution.py:96
  136.5 3.1 gather_fusion.3
  149.4 3.0 copy.84
  152.4 7.1 %copy.62 = bf16[8,128,12,64]{3,0,2,1:T(8,128)(2,1)} copy(bf16[8,128,12,64]{1,0,3,2:T(8,128)(2,1)} %bitcast.204) | data formatting | bytes 3145728 | tf_op jit(solution)/shard_map/reshape;reshape;squeeze | solution.py:96
  159.6 3.2 gather_fusion.4
  164.9 88.0 %all_gather.7 = bf16[256,768]{1,0:T(8,128)(2,1)} all-gather(bf16[8,768]{1,0:T(8,128)(2,1)S(1)} %reshape.58), channel_id=1, replica_groups=mesh['seq'=32,'rep'=4] {'seq'}, dimensions={0}, use_global_device_ids=true | all-gather | bytes 405504 | tf_op jit(solution)/shard_map/all_gather | solution.py:119
  270.8 4.3 fusion.38
  275.9 127.4 %while.14 = (s32[]{:T(128)}, f32[12,1024,64]{1,2,0:T(8,128)}, f32[12,1024,64]{1,2,0:T(8,128)}, f32[12,1024,64]{1,2,0:T(8,128)}, bf16[12,1024,64]{1,2,0:T(8,128)(...) while((s32[]{:T(128)}, f32[12,1024,64]{1,2,0:T(8,128)}, ...), condition=%wide.region_2.0_spmd, body=%wide.region_1.0_spmd.sunk | while | flops 679608320 | bytes 20612216 | solution.py:82
  403.6 3.5 broadcast.23.clone
  409.1 7.0 %copy.66 = f32[8,128,12,64]{1,0,3,2:T(8,128)} copy(f32[8,128,12,64]{3,0,2,1:T(8,128)} %scatter_fusion) | data formatting | bytes 6291456 | tf_op jit(solution)/shard_map/scatter | solution.py:153
  419.0 3.6 fusion.37
  426.0 37.3 %reduce-scatter.4.cloned.1.call-done = f32[8,768]{1,0:T(8,128)} async-done(((f32[256,768]{1,0:T(8,128)}), f32[8,768]{1,0:T(8,128)}) %reduce-scatter.4.cloned.1.call-update) | async-done | bytes 24592 | tf_op jit(solution)/shard_map/reduce_scatter | solution.py:143
  464.1 3.4 broadcast.23.clone.1
  469.6 5.7 copy.72
  477.7 3.4 broadcast.23.clone.2
  483.2 5.7 copy.69
  491.2 134.1 %reduce-scatter.8.cloned.1.call-done = f32[24,768]{1,0:T(8,128)} async-done(((f32[768,768]{1,0:T(8,128)}), f32[24,768]{1,0:T(8,128)}) %reduce-scatter.8.cloned.1.call-update) | async-done | bytes 73744 | tf_op jit(solution)/shard_map/reduce_scatter | solution.py:28
  625.4 6.9 %fusion.35 = (bf16[1024,12,64]{0,2,1:T(8,128)(2,1)}, bf16[1024,12,64]{0,2,1:T(8,128)(2,1)S(1)}) fusion(f32[1024,12,64]{0,2,1:T(8,128)} %reshape.67, f32[12,1024,64]{1,2,0:T(8,128)} %get-tuple-element.60, f32[1024,12,64]{0,2,1:T(8,128)} %reshape.64, f32[12,1024,64]{1,2,0:T(8,128)} %get-tuple-element.59), kind=kLoop, calls=%fused_computation.47 | loop fusion | flops 3145728 | bytes 15728640 | tf_op jit(solution)/shard_map/convert_element_type | solution.py:159
  636.5 29.3 %all-reduce.2.cloned.1.call-done = f32[24,768]{1,0:T(8,128)} async-done(((f32[24,768]{1,0:T(8,128)}), f32[24,768]{1,0:T(8,128)}) %all-reduce.2.cloned.1.call-update) | async-done | bytes 73744 | tf_op jit(solution)/shard_map/psum | solution.py:36
  (144 shorter events, 199.1 us)
Async XLA Ops:
  7.2 116.8 %copy-start = (bf16[1,1024,768]{2,1,0:T(8,128)(2,1)S(1)}, bf16[1,1024,768]{2,1,0:T(8,128)(2,1)}, u32[]{:S(2)}) copy-start(bf16[1,1024,768]{2,1,0:T(8,128)(2,1)} %param.14) | copy-start | bytes 4718596
  7.2 417.9 %reduce-scatter.6.cloned.1.call-start = ((), (), s32[]{:S(2)}) async-start(), calls=%async_computation.4 | async-start | bytes 811008 | tf_op jit(solution)/shard_map/reduce_scatter | solution.py:144
  126.6 1.1 copy-start.2
  141.9 0.6 copy-start.3
  146.8 316.4 %reduce-scatter.4.cloned.1.call-start = ((), (), s32[]{:S(2)}) async-start(), calls=%async_computation.3 | async-start | bytes 811008 | tf_op jit(solution)/shard_map/reduce_scatter | solution.py:143
  260.0 0.6 copy-start.6
  265.8 0.6 copy-start.4
  270.7 354.6 %reduce-scatter.8.cloned.1.call-start = ((), (), s32[]{:S(2)}) async-start(), calls=%async_computation.5 | async-start | bytes 2433024 | tf_op jit(solution)/shard_map/reduce_scatter | solution.py:28
  275.0 390.8 %all-reduce.2.cloned.1.call-start = ((), (), s32[]{:S(2)}) async-start(), calls=%async_computation.6 | async-start | bytes 147456 | tf_op jit(solution)/shard_map/psum | solution.py:36
  275.9 127.5 %copy-start.5 = (bf16[12,8,256]{2,1,0:T(8,128)(2,1)S(1)}, bf16[12,8,256]{2,1,0:T(8,128)(2,1)}, u32[]{:S(2)}) copy-start(bf16[12,8,256]{2,1,0:T(8,128)(2,1)} %copy-done.4) | copy-start | bytes 147460
  632.3 35.1 %copy-start.1 = (bf16[1,1024,768]{2,1,0:T(8,128)(2,1)S(1)}, bf16[1,1024,768]{2,1,0:T(8,128)(2,1)}, u32[]{:S(2)}) copy-start(bf16[1,1024,768]{2,1,0:T(8,128)(2,1)} %param.14) | copy-start | bytes 4718596
Sparse Core Ops, SparseCore 0:
  146.9 156.7 reduce-scatter.5
  306.2 156.9 reduce-scatter.3
  465.6 159.6 reduce-scatter.7
  627.7 38.0 all-reduce.1
where the time goes:
time: 681 us; the launch traced here: 674 us
  waiting for transfers between devices  201 us (30%)
  blocking collectives  173 us (25%)
  local copies, waits for them, and re-layouts  141 us (21%)
  matrix products  131 us (19%)
  other arithmetic  14.6 us (2%)
  between operations  14 us (2%)
    reduce_scatter x1, waiting for transfers between devices, on_device(): lax.psum_scatter(lax.dot_general(saved_mat, grad_mat, (((0,), (0,)), ((),...  134 us
    all_gather x1, blocking collectives, on_device(): lax.all_gather(join_heads(dilated_value), 'seq', axis=0, tiled=True)  88 us
    all_gather x1, blocking collectives, on_device(): lax.all_gather(join_heads(dilated_key), 'seq', axis=0, tiled=True)  84.5 us
    reduce_scatter x1, waiting for transfers between devices, on_device(): lax.psum_scatter(join_heads(grad_k), 'seq', scatter_dimension=0, tiled=True)  37.3 us
    dot_general x12, matrix products, one_head(): lax.dot_general(weight_matrix, head_grad, (((0,), (0,)), ((), ())), prefe...  30.3 us
    unnamed x27, local copies, waits for them, and re-layouts  29.4 us
    psum x1, waiting for transfers between devices, on_device(): weight_sum = lax.psum(shard_sum, 'rep')  29.3 us
    dot_general x12, matrix products, one_head(): jnp.dot(scores_gradient, head_key, preferred_element_type=jnp.float32)  28.5 us
  transfers between devices with their start and end apart: 4, of which 3 were waited for; matrix products, arithmetic and copies ran while one was open for 34% of the time, Pallas kernels for 0%

commit v1 on v0

v1 whole, which is shorter than its diff:
```python
import functools
import math

import jax
import jax.numpy as jnp
from jax import lax
from jax.experimental import pallas as pl
from jax.experimental.pallas import tpu as pltpu
from jax.sharding import PartitionSpec as P

F32 = jnp.float32
BF16 = jnp.bfloat16
DIL = 128
HEADS = 12
HW = 64
D = HEADS * HW
SUB = 16
LOG2E = math.log2(math.e)
SCALE = HW ** -0.5
STAT = 2 * D
PROJ = STAT + 128
VMEM = 60 * 2 ** 20


def dot(a, b, ca, cb):
    return lax.dot_general(a, b, (((ca,), (cb,)), ((), ())), preferred_element_type=F32)


def iota(shape, axis):
    return lax.broadcasted_iota(jnp.int32, shape, axis)


def head_rows(rows):
    keep = iota((1, SUB, D), 1) == iota((1, SUB, D), 2) // HW
    return jnp.sum(jnp.where(keep, rows.astype(F32), 0.0), axis=1)


def three_terms(x):
    x = jnp.where(iota(x.shape, 1) < HEADS, x, 0.0)
    hi = x.astype(BF16).astype(F32)
    mid = (x - hi).astype(BF16).astype(F32)
    low = ((x - hi) - mid).astype(BF16).astype(F32)
    return hi + pltpu.roll(mid, 16, 1) + pltpu.roll(low, 32, 1)


def join_terms(x):
    return (x + pltpu.roll(x, 112, 1)) + pltpu.roll(x, 96, 1)


def front_kernel(steps, seq, saved_ref, grad_ref, w_ref, lse_ref, q_ref, k_ref, v_ref,
                 attn_ref, delta_ref, send_ref, acc, gsel, dsel):
    step = pl.program_id(0)
    saved = saved_ref[...]
    grad = grad_ref[...]
    rows = saved.shape[0]
    attn = dot(grad, w_ref[...], 1, 1).astype(BF16)
    attn_ref[...] = attn
    attn_f = attn.astype(F32)
    term = dot(saved, grad, 0, 0)

    @pl.when(step == 0)
    def _():
        acc[...] = term

    @pl.when(step > 0)
    def _():
        acc[...] += term

    prod = attn_f * saved.astype(F32)
    hi = prod.astype(BF16)
    low = (prod - hi.astype(F32)).astype(BF16)
    pick = (iota((D, 128), 0) // HW == iota((D, 128), 1)).astype(BF16)
    delta = dot(hi, pick, 1, 0) + dot(low, pick, 1, 0)
    delta_ref[...] = delta.T[:SUB]
    groups = rows // DIL
    grouped = attn_f.reshape(groups, DIL, D)[:, :SUB]
    picked = head_rows(grouped)
    diag = iota((1, DIL, 128), 1) == iota((1, DIL, 128), 2)
    dpicked = jnp.sum(jnp.where(diag, delta.reshape(groups, DIL, 128), 0.0), axis=1)
    for i in range(groups):
        gsel[pl.ds(step * groups + i, 1), :] = picked[i:i + 1]
        dsel[pl.ds(step * groups + i, 1), :] = dpicked[i:i + 1]

    @pl.when(step == steps - 1)
    def _():
        diag = iota((HEADS, 128), 0) == iota((HEADS, 128), 1)
        lse = jnp.concatenate(
            [jnp.sum(jnp.where(diag, lse_ref[:, DIL * j:DIL * (j + 1)], 0.0), axis=0, keepdims=True)
             for j in range(8)], axis=0)
        top = jnp.concatenate([head_rows(q_ref[...]), head_rows(k_ref[...]), three_terms(lse)], axis=1)
        bot = jnp.concatenate([head_rows(v_ref[...]), gsel[...], three_terms(dsel[...])], axis=1)
        own = jnp.concatenate([top, bot], axis=0).astype(BF16)
        share = D // seq
        for s in range(seq):
            send_ref[s, :, 0:PROJ] = own
            send_ref[s, :, PROJ:PROJ + D] = acc[share * s:share * s + 16].astype(BF16)
            rest = acc[share * s + 16:share * s + 24]
            send_ref[s, :, PROJ + D:PROJ + D + D // 2] = jnp.concatenate(
                [rest[:, :D // 2], rest[:, D // 2:]], axis=0).astype(BF16)


def front(saved, grad, w, lse, q, k, v, seq):
    tok = saved.shape[0]
    steps = 4
    rows = tok // steps
    row_spec = pl.BlockSpec((rows, D), lambda i: (i, 0))
    sel_spec = pl.BlockSpec((tok // DIL, SUB, D), lambda i: (0, 0, 0))
    view = lambda x: x.reshape(tok // DIL, DIL, D)
    return pl.pallas_call(
        functools.partial(front_kernel, steps, seq),
        grid=(steps,),
        in_specs=[row_spec, row_spec,
                  pl.BlockSpec((D, D), lambda i: (0, 0)),
                  pl.BlockSpec((HEADS, tok), lambda i: (0, 0)),
                  sel_spec, sel_spec, sel_spec],
        out_specs=[row_spec,
                   pl.BlockSpec((SUB, rows), lambda i: (0, i)),
                   pl.BlockSpec((seq, 16, PROJ + D + D // 2), lambda i: (0, 0, 0))],
        out_shape=[jax.ShapeDtypeStruct((tok, D), BF16),
                   jax.ShapeDtypeStruct((SUB, tok), F32),
                   jax.ShapeDtypeStruct((seq, 16, PROJ + D + D // 2), BF16)],
        scratch_shapes=[pltpu.VMEM((D, D), F32),
                        pltpu.VMEM((tok // DIL, D), F32),
                        pltpu.VMEM((tok // DIL, 128), F32)],
        compiler_params=pltpu.CompilerParams(vmem_limit_bytes=VMEM),
        cost_estimate=pl.CostEstimate(flops=4 * tok * D * D, bytes_accessed=9 * 10 ** 6, transcendentals=0),
    )(saved, grad, w, lse, view(q), view(k), view(v))


def local_kernel(chunk, q_ref, k_ref, v_ref, g_ref, lse_ref, delta_ref,
                 dq_ref, dk_ref, dv_ref, sq_ref, sk_ref, sv_ref):
    pair = pl.program_id(0)
    q2, k2, v2, g2 = q_ref[...], k_ref[...], v_ref[...], g_ref[...]
    tok = q2.shape[0]
    lane = iota((1, 128), 1)
    k_turned = k2.T
    zero = jnp.zeros((), BF16)
    qm = [jnp.where(lane < HW, q2, zero), jnp.where(lane >= HW, q2, zero)]
    gm = [jnp.where(lane < HW, g2, zero), jnp.where(lane >= HW, g2, zero)]
    grad_k = grad_v = None
    grad_q = []
    for c in range(tok // chunk):
        part = slice(c * chunk, (c + 1) * chunk)
        turned = []
        for h in range(2):
            qc, gc = qm[h][part], gm[h][part]
            lse = lse_ref[pl.ds(2 * pair + h, 1), part] * LOG2E
            delta = delta_ref[pl.ds(2 * pair + h, 1), part]
            prob = jnp.exp2(dot(k2, qc, 1, 1) * (SCALE * LOG2E) - lse)
            dscore = (prob * (dot(v2, gc, 1, 1) - delta)).astype(BF16)
            weight = prob.astype(BF16)
            a, b = dot(dscore, qc, 1, 0), dot(weight, gc, 1, 0)
            grad_k = a if grad_k is None else grad_k + a
            grad_v = b if grad_v is None else grad_v + b
            turned.append(dot(k_turned[HW * h:HW * h + HW], dscore, 1, 0))
        grad_q.append(jnp.concatenate(turned, axis=0).T)
    grad_q = jnp.concatenate(grad_q, axis=0) * SCALE
    grad_k = grad_k * SCALE
    groups = tok // DIL
    keep = iota((1, DIL, 128), 1) == 2 * pair + iota((1, DIL, 128), 2) // HW
    for out, sel, val in ((dq_ref, sq_ref, grad_q), (dk_ref, sk_ref, grad_k), (dv_ref, sv_ref, grad_v)):
        out[...] = val.astype(BF16)
        sel[...] = jnp.sum(jnp.where(keep, val.reshape(groups, DIL, 128), 0.0), axis=1)


def local_level(q, k, v, g, lse, delta):
    tok = q.shape[0]
    pairs = HEADS // 2
    col = pl.BlockSpec((tok, 128), lambda i: (0, i))
    sel = pl.BlockSpec((tok // DIL, 128), lambda i: (0, i))
    return pl.pallas_call(
        functools.partial(local_kernel, 256),
        grid=(pairs,),
        in_specs=[col] * 4 + [pl.BlockSpec((HEADS, tok), lambda i: (0, 0)),
                              pl.BlockSpec((SUB, tok), lambda i: (0, 0))],
        out_specs=[col] * 3 + [sel] * 3,
        out_shape=[jax.ShapeDtypeStruct((tok, D), BF16)] * 3
        + [jax.ShapeDtypeStruct((tok // DIL, D), F32)] * 3,
        compiler_params=pltpu.CompilerParams(vmem_limit_bytes=VMEM),
        cost_estimate=pl.CostEstimate(flops=10 * HEADS * tok * tok * HW * 2, bytes_accessed=11 * 10 ** 6,
                                      transcendentals=HEADS * tok * tok),
    )(q, k, v, g, lse, delta)


def last_kernel(recv_ref, own_ref, sq_ref, sk_ref, sv_ref, dq_in, dk_in, dv_in, dq_ref, dk_ref, dv_ref):
    every = recv_ref[...].astype(F32)
    count = every.shape[0] * 8
    top = every[:, :8].reshape(count, PROJ)
    bot = every[:, 8:].reshape(count, PROJ)
    q, k = top[:, :D].astype(BF16), top[:, D:2 * D].astype(BF16)
    v, g = bot[:, :D].astype(BF16), bot[:, D:2 * D].astype(BF16)
    lse = join_terms(top[:, STAT:]).T[:HEADS]
    delta = join_terms(bot[:, STAT:]).T[:HEADS]
    own = own_ref[0].astype(F32)
    own_head = iota((HEADS, 8, D), 0) == iota((HEADS, 8, D), 2) // HW

    def by_head(x):
        return jnp.where(own_head, jnp.broadcast_to(x[None], (HEADS, 8, D)), 0.0).reshape(HEADS * 8, D).astype(BF16)

    def column(x):
        x = jnp.broadcast_to(join_terms(x)[None], (HEADS, 8, 128))
        x = jnp.where(iota(x.shape, 0) == iota(x.shape, 2), x, 0.0)
        return jnp.sum(x.reshape(HEADS * 8, 128), axis=1, keepdims=True)

    def row(x):
        return jnp.broadcast_to(x[:, None], (HEADS, 8, count)).reshape(HEADS * 8, count)

    def back(x):
        return jnp.sum(jnp.where(own_head, x.reshape(HEADS, 8, D), 0.0), axis=0)

    def pieces(left_s, right_s, left_p, right_p, lse, delta):
        prob = jnp.exp2(dot(left_s, right_s, 1, 1) * (SCALE * LOG2E) - lse * LOG2E)
        dscore = (prob * (dot(left_p, right_p, 1, 1) - delta)).astype(BF16)
        return prob.astype(BF16), dscore

    _, dscore = pieces(by_head(own[:8, :D]), k, by_head(own[8:, D:2 * D]), v,
                       column(own[:8, STAT:]), column(own[8:, STAT:]))
    grad_q = back(dot(dscore, k, 1, 0)) * SCALE
    weight, dscore = pieces(by_head(own[:8, D:2 * D]), q, by_head(own[8:, :D]), g, row(lse), row(delta))
    grad_k = back(dot(dscore, q, 1, 0)) * SCALE
    grad_v = back(dot(weight, g, 1, 0))
    here = iota((8, SUB, D), 1) == iota((8, SUB, D), 2) // HW
    for sel, grad, old, out in ((sq_ref, grad_q, dq_in, dq_ref), (sk_ref, grad_k, dk_in, dk_ref),
                                (sv_ref, grad_v, dv_in, dv_ref)):
        total = sel[...] + grad
        out[...] = jnp.where(here, jnp.broadcast_to(total[:, None], (8, SUB, D)),
                             old[...].astype(F32)).astype(BF16)


def last(recv, send, sums, grads):
    seq = recv.shape[0]
    tok = grads[0].shape[0]
    sub = pl.BlockSpec((tok // DIL, SUB, D), lambda i: (0, 0, 0))
    sel = pl.BlockSpec((tok // DIL, D), lambda i: (0, 0))
    view = jax.ShapeDtypeStruct((tok // DIL, DIL, D), BF16)
    return pl.pallas_call(
        last_kernel,
        grid=(1,),
        in_specs=[pl.BlockSpec((seq, 16, PROJ), lambda i: (0, 0, 0)),
                  pl.BlockSpec((1, 16, PROJ), lambda i: (0, 0, 0))] + [sel] * 3 + [sub] * 3,
        out_specs=[sub] * 3,
        out_shape=[view] * 3,
        input_output_aliases={5: 0, 6: 1, 7: 2},
        compiler_params=pltpu.CompilerParams(vmem_limit_bytes=VMEM),
        cost_estimate=pl.CostEstimate(flops=7 * 2 * 96 * 256 * D, bytes_accessed=4 * 10 ** 6,
                                      transcendentals=2 * 96 * 256),
    )(recv, send, *sums, *[x.reshape(view.shape) for x in grads])


def on_device(queries, key_rows, value_rows, saved_out, logsumexp, out_grad, proj_weight):
    q, k, v = queries[0], key_rows[0], value_rows[0]
    lse = logsumexp[0]
    tok = q.shape[0]
    seq = lax.axis_size("seq")
    rep = lax.axis_size("rep")
    attn, delta, send = front(saved_out[0], out_grad[0], proj_weight, lse, q, k, v, seq)
    recv = lax.all_to_all(send, "seq", 0, 0)
    *grads, sq, sk, sv = local_level(q, k, v, attn, lse, delta)
    total = jnp.sum(recv[:, :, PROJ:].astype(F32), axis=0)
    rest = total[:, D:]
    mine = jnp.concatenate([total[:, :D], jnp.concatenate([rest[:8], rest[8:]], axis=1)], axis=0)

    def other(x, bit):
        return lax.ppermute(x, "rep", [(i, i ^ bit) for i in range(rep)])

    pair_sum = mine + other(mine, 2)
    all_sum = pair_sum + other(pair_sum, 1)
    projection_gradient = all_sum * (1.0 / math.sqrt(rep * seq * tok))
    outs = last(recv, send, (sq, sk, sv), grads)
    return (*[x.reshape(1, tok, D) for x in outs], projection_gradient)


def solution(mesh):
    rows = P("rep", "seq", None)
    return jax.shard_map(
        on_device,
        mesh=mesh,
        in_specs=(rows, rows, rows, rows, P("rep", None, "seq"), rows, P()),
        out_specs=(rows, rows, rows, P("seq", None)),
        check_vma=False,
    )
```

time: 681 us -> 104 us (0.15)
  the two profiles are of different devices: /device:TPU:2 before, /device:TPU:1 now
where the time goes in v1:
time: 104 us
  Pallas kernels  47.5 us (46%)
  blocking collectives  44.8 us (43%)
  starting transfers between devices  6.36 us (6%)
  waiting for transfers between devices  2.09 us (2%)
  local copies, waits for them, and re-layouts  1.45 us (1%)
    all_to_all x1, blocking collectives, on_device(): recv = lax.all_to_all(send, 'seq', 0, 0)  44.8 us
    pallas_call x1, Pallas kernels, local_level(): pl.pallas_call(functools.partial(local_kernel, 256), grid=(pairs,), in_sp...  34.2 us
    pallas_call x1, Pallas kernels, front(): pl.pallas_call(functools.partial(front_kernel, steps, seq), grid=(steps,)...  9.78 us
    ppermute x2, starting transfers between devices, other(): return lax.ppermute(x, 'rep', [(i, i ^ bit) for i in range(rep)])  6.36 us
    pallas_call x1, Pallas kernels, last(): pl.pallas_call(last_kernel, grid=(1,), in_specs=[pl.BlockSpec((seq, 16, P...  3.52 us
    ppermute x2, waiting for transfers between devices, other(): return lax.ppermute(x, 'rep', [(i, i ^ bit) for i in range(rep)])  2.09 us
  transfers between devices with their start and end apart: 2, of which 1 were waited for; matrix products, arithmetic and copies ran while one was open for 0% of the time, Pallas kernels for 36%

profile of v1, /device:TPU:1, one launch (start us, length us, event | category | flops | bytes accessed | tf_op | source)
XLA Modules:
  0.0 103.8 jit_solution(1972549189552946676)
XLA Ops:
  0.6 1.4 %copy.16 = f32[1,12,1024]{2,1,0:T(8,128)} copy(f32[1,12,1024]{2,0,1:T(1,128)} %param.11) | data formatting | bytes 98304
  2.1 9.8 %shard_map.102 = (bf16[1024,768]{1,0:T(8,128)(2,1)}, f32[16,1024]{1,0:T(8,128)}, bf16[32,16,2816]{2,1,0:T(8,128)(2,1)}) custom-call(bf16[1024,768]{1,0:T(8,128)(2,1)} %bitcast.17, bf16[1024,768]{1,0:T(8,128)(2,1)} %bitcast.18, bf16[768,768]{1,0:T(8,128)(2,1)} %w_ref.1, f32[12,1024]{1,0:T(8,128)} %bitcast.31, bf16[8,128,768]{2,1,0:T(8,128)(2,1)} %bitcast.19, ...), custom_call_target="tpu_custom_call" | custom-call | flops 2415919104 | bytes 9000000 | tf_op jit(solution)/shard_map/pallas_call | solution.py:109
  11.9 44.8 %all_to_all.5.recv_ref = bf16[32,16,2816]{2,1,0:T(8,128)(2,1)S(1)} all-to-all(bf16[32,16,2816]{2,1,0:T(8,128)(2,1)} %get-tuple-element.16.own_ref), channel_id=1, replica_groups=mesh['seq'=32,'rep'=4] {'seq'}, dimensions={0} | all-to-all | bytes 5767168 | tf_op jit(solution)/shard_map/all_to_all | solution.py:257
  56.7 0.0 copy-start
  56.7 0.2 convert_reduce_fusion
  56.9 2.7 %collective-permute-start = (f32[24,768]{1,0:T(8,128)S(1)}, f32[24,768]{1,0:T(8,128)S(1)}, u32[]{:S(2)}, u32[]{:S(2)}) collective-permute-start(f32[24,768]{1,0:T(8,128)S(1)} %maximum_maximum_fusion), channel_id=1, source_target_pairs={{0,2},{1,3},{2,0},{3,1},{4,6},{5,7},{6,4},{7,5},{8,10},{9,11},{10,... | collective-permute-start | bytes 221192 | tf_op jit(solution)/shard_map/ppermute | solution.py:264
  59.6 2.1 %collective-permute-done = f32[24,768]{1,0:T(8,128)S(1)} collective-permute-done((f32[24,768]{1,0:T(8,128)S(1)}, f32[24,768]{1,0:T(8,128)S(1)}, u32[]{:S(2)}, u32[]{:S(2)}) %collective-permute-start) | collective-permute-done | bytes 73760 | tf_op jit(solution)/shard_map/ppermute | solution.py:264
  61.7 3.7 %collective-permute-start.1 = (f32[24,768]{1,0:T(8,128)S(1)}, f32[24,768]{1,0:T(8,128)S(1)}, u32[]{:S(2)}, u32[]{:S(2)}) collective-permute-start(f32[24,768]{1,0:T(8,128)S(1)} %fusion), channel_id=1, source_target_pairs={{0,1},{1,0},{2,3},{3,2},{4,5},{5,4},{6,7},{7,6},{8,9},{9,8},{10,11... | collective-permute-start | bytes 221192 | tf_op jit(solution)/shard_map/ppermute | solution.py:264
  65.3 34.2 %shard_map.103 = (bf16[1024,768]{1,0:T(8,128)(2,1)}, bf16[1024,768]{1,0:T(8,128)(2,1)}, bf16[1024,768]{1,0:T(8,128)(2,1)}, f32[8,768]{1,0:T(8,128)}, f32[8,768]{1,0:T(8,128)}, /*index=5*/f32[8,768]{1,0:T(8,128)}) custom-call(bf16[1024,768]{1,0:T(8,128)(2,1)} %bitcast.20, bf16[1024,768]{1,0:T(8,128)(2,1)} %bitcast.22, bf16[1024,768]{1,0:T(8,128)(2,1)} %bitcast.24, ...), custom_call_target="tpu_custom_call" | custom-call | flops 16106127360 | bytes 11000000 | tf_op jit(solution)/shard_map/pallas_call | solution.py:171
  99.6 0.0 copy-done
  99.6 3.5 %shard_map.104 = (bf16[8,128,768]{2,1,0:T(8,128)(2,1)}, bf16[8,128,768]{2,1,0:T(8,128)(2,1)}, bf16[8,128,768]{2,1,0:T(8,128)(2,1)}) custom-call(bf16[32,16,2816]{2,1,0:T(8,128)(2,1)} %copy-done, bf16[32,16,2816]{2,1,0:T(8,128)(2,1)} %get-tuple-element.16.own_ref, ...), custom_call_target="tpu_custom_call", output_to_operand_aliasing={{0}: (5, {}), {1}: (6, {}), {2}: (7, {})} | custom-call | flops 264241152 | bytes 4000000 | tf_op jit(solution)/shard_map/pallas_call | solution.py:236
  103.1 0.0 collective-permute-done.1
  103.1 0.6 add_multiply_fusion
  (4 shorter events, 0.0 us)
Async XLA Ops:
  56.7 42.9 %copy-start = (bf16[32,16,2816]{2,1,0:T(8,128)(2,1)}, bf16[32,16,2816]{2,1,0:T(8,128)(2,1)S(1)}, u32[]{:S(2)}) copy-start(bf16[32,16,2816]{2,1,0:T(8,128)(2,1)S(1)} %all_to_all.5.recv_ref) | copy-start | bytes 8650756
  56.9 4.8 %collective-permute-start = (f32[24,768]{1,0:T(8,128)S(1)}, f32[24,768]{1,0:T(8,128)S(1)}, u32[]{:S(2)}, u32[]{:S(2)}) collective-permute-start(f32[24,768]{1,0:T(8,128)S(1)} %maximum_maximum_fusion), channel_id=1, source_target_pairs={{0,2},{1,3},{2,0},{3,1},{4,6},{5,7},{6,4},{7,5},{8,10},{9,11},{10,... | collective-permute-start | bytes 221192 | tf_op jit(solution)/shard_map/ppermute | solution.py:264
  61.7 41.4 %collective-permute-start.1 = (f32[24,768]{1,0:T(8,128)S(1)}, f32[24,768]{1,0:T(8,128)S(1)}, u32[]{:S(2)}, u32[]{:S(2)}) collective-permute-start(f32[24,768]{1,0:T(8,128)S(1)} %fusion), channel_id=1, source_target_pairs={{0,1},{1,0},{2,3},{3,2},{4,5},{5,4},{6,7},{7,6},{8,9},{9,8},{10,11... | collective-permute-start | bytes 221192 | tf_op jit(solution)/shard_map/ppermute | solution.py:264

commit v2 on v1

--- a/solution.py
+++ b/solution.py
@@ -19,7 +19,8 @@
 SCALE = HW ** -0.5
 STAT = 2 * D
 PROJ = STAT + 128
-VMEM = 60 * 2 ** 20
+TERM = D + D // 2
+VMEM = 62 * 2 ** 20
 
 
 def dot(a, b, ca, cb):
@@ -83,9 +84,9 @@
 
     @pl.when(step == steps - 1)
     def _():
-        diag = iota((HEADS, 128), 0) == iota((HEADS, 128), 1)
+        lane = iota((1, 128), 1)
         lse = jnp.concatenate(
-            [jnp.sum(jnp.where(diag, lse_ref[:, DIL * j:DIL * (j + 1)], 0.0), axis=0, keepdims=True)
+            [sum(jnp.where(lane == h, lse_ref[h, :, DIL * j:DIL * (j + 1)], 0.0) for h in range(HEADS))
              for j in range(8)], axis=0)
         top = jnp.concatenate([head_rows(q_ref[...]), head_rows(k_ref[...]), three_terms(lse)], axis=1)
         bot = jnp.concatenate([head_rows(v_ref[...]), gsel[...], three_terms(dsel[...])], axis=1)
@@ -95,7 +96,7 @@
             send_ref[s, :, 0:PROJ] = own
             send_ref[s, :, PROJ:PROJ + D] = acc[share * s:share * s + 16].astype(BF16)
             rest = acc[share * s + 16:share * s + 24]
-            send_ref[s, :, PROJ + D:PROJ + D + D // 2] = jnp.concatenate(
+            send_ref[s, :, PROJ + D:] = jnp.concatenate(
                 [rest[:, :D // 2], rest[:, D // 2:]], axis=0).astype(BF16)
 
 
@@ -111,14 +112,14 @@
         grid=(steps,),
         in_specs=[row_spec, row_spec,
                   pl.BlockSpec((D, D), lambda i: (0, 0)),
-                  pl.BlockSpec((HEADS, tok), lambda i: (0, 0)),
+                  pl.BlockSpec((HEADS, 1, tok), lambda i: (0, 0, 0)),
                   sel_spec, sel_spec, sel_spec],
         out_specs=[row_spec,
                    pl.BlockSpec((SUB, rows), lambda i: (0, i)),
-                   pl.BlockSpec((seq, 16, PROJ + D + D // 2), lambda i: (0, 0, 0))],
+                   pl.BlockSpec((seq, 16, PROJ + TERM), lambda i: (0, 0, 0))],
         out_shape=[jax.ShapeDtypeStruct((tok, D), BF16),
                    jax.ShapeDtypeStruct((SUB, tok), F32),
-                   jax.ShapeDtypeStruct((seq, 16, PROJ + D + D // 2), BF16)],
+                   jax.ShapeDtypeStruct((seq, 16, PROJ + TERM), BF16)],
         scratch_shapes=[pltpu.VMEM((D, D), F32),
                         pltpu.VMEM((tok // DIL, D), F32),
                         pltpu.VMEM((tok // DIL, 128), F32)],
@@ -127,9 +128,9 @@
     )(saved, grad, w, lse, view(q), view(k), view(v))
 
 
-def local_kernel(chunk, q_ref, k_ref, v_ref, g_ref, lse_ref, delta_ref,
-                 dq_ref, dk_ref, dv_ref, sq_ref, sk_ref, sv_ref):
-    pair = pl.program_id(0)
+def local_kernel(chunk, first, q_ref, k_ref, v_ref, g_ref, lse_ref, delta_ref, *rest):
+    dq_ref, dk_ref, dv_ref, sq_ref, sk_ref, sv_ref = rest[-6:]
+    pair = first + pl.program_id(0)
     q2, k2, v2, g2 = q_ref[...], k_ref[...], v_ref[...], g_ref[...]
     tok = q2.shape[0]
     lane = iota((1, 128), 1)
@@ -144,7 +145,7 @@
         turned = []
         for h in range(2):
             qc, gc = qm[h][part], gm[h][part]
-            lse = lse_ref[pl.ds(2 * pair + h, 1), part] * LOG2E
+            lse = lse_ref[2 * pair + h, :, part] * LOG2E
             delta = delta_ref[pl.ds(2 * pair + h, 1), part]
             prob = jnp.exp2(dot(k2, qc, 1, 1) * (SCALE * LOG2E) - lse)
             dscore = (prob * (dot(v2, gc, 1, 1) - delta)).astype(BF16)
@@ -163,26 +164,64 @@
         sel[...] = jnp.sum(jnp.where(keep, val.reshape(groups, DIL, 128), 0.0), axis=1)
 
 
-def local_level(q, k, v, g, lse, delta):
+def local_level(first, count, q, k, v, g, lse, delta, before=(), after=None):
     tok = q.shape[0]
-    pairs = HEADS // 2
-    col = pl.BlockSpec((tok, 128), lambda i: (0, i))
-    sel = pl.BlockSpec((tok // DIL, 128), lambda i: (0, i))
-    return pl.pallas_call(
-        functools.partial(local_kernel, 256),
-        grid=(pairs,),
-        in_specs=[col] * 4 + [pl.BlockSpec((HEADS, tok), lambda i: (0, 0)),
-                              pl.BlockSpec((SUB, tok), lambda i: (0, 0))],
+    col = pl.BlockSpec((tok, 128), lambda i: (0, first + i))
+    sel = pl.BlockSpec((tok // DIL, 128), lambda i: (0, first + i))
+    extra = list(before) + ([] if after is None else [after])
+    return pl.pallas_call(
+        functools.partial(local_kernel, 256, first),
+        grid=(count,),
+        in_specs=[col] * 4 + [pl.BlockSpec((HEADS, 1, tok), lambda i: (0, 0, 0)),
+                              pl.BlockSpec((SUB, tok), lambda i: (0, 0))]
+        + [pl.BlockSpec(memory_space=pl.ANY)] * len(extra),
         out_specs=[col] * 3 + [sel] * 3,
         out_shape=[jax.ShapeDtypeStruct((tok, D), BF16)] * 3
         + [jax.ShapeDtypeStruct((tok // DIL, D), F32)] * 3,
+        input_output_aliases={6 + i: i for i in range(len(before))},
         compiler_params=pltpu.CompilerParams(vmem_limit_bytes=VMEM),
-        cost_estimate=pl.CostEstimate(flops=10 * HEADS * tok * tok * HW * 2, bytes_accessed=11 * 10 ** 6,
-                                      transcendentals=HEADS * tok * tok),
-    )(q, k, v, g, lse, delta)
-
-
-def last_kernel(recv_ref, own_ref, sq_ref, sk_ref, sv_ref, dq_in, dk_in, dv_in, dq_ref, dk_ref, dv_ref):
+        cost_estimate=pl.CostEstimate(flops=20 * count * tok * tok * HW * 2, bytes_accessed=2 * count * 10 ** 6,
+                                      transcendentals=2 * count * tok * tok),
+    )(q, k, v, g, lse, delta, *extra)
+
+
+def add_kernel(a_ref, b_ref, after, out_ref):
+    out_ref[...] = a_ref[...] + b_ref[...]
+
+
+def add_after(a, b, after):
+    whole = pl.BlockSpec(a.shape, lambda: (0, 0))
+    return pl.pallas_call(
+        add_kernel,
+        in_specs=[whole, whole, pl.BlockSpec(memory_space=pl.ANY)],
+        out_specs=whole,
+        out_shape=jax.ShapeDtypeStruct(a.shape, a.dtype),
+        cost_estimate=pl.CostEstimate(flops=a.size, bytes_accessed=12 * a.size, transcendentals=0),
+    )(a, b, after)
+
+
+def terms_kernel(recv_ref, after, out_ref):
+    total = jnp.sum(recv_ref[...].astype(F32), axis=0)
+    out_ref[:16] = total[:, :D]
+    out_ref[16:, :D // 2] = total[:8, D:]
+    out_ref[16:, D // 2:] = total[8:, D:]
+
+
+def sum_terms(recv, after):
+    seq = recv.shape[0]
+    return pl.pallas_call(
+        terms_kernel,
+        grid=(1,),
+        in_specs=[pl.BlockSpec((pl.Element(seq), pl.Element(16), pl.Element(TERM)), lambda i: (0, 0, PROJ)),
+                  pl.BlockSpec(memory_space=pl.ANY)],
+        out_specs=pl.BlockSpec((24, D), lambda i: (0, 0)),
+        out_shape=jax.ShapeDtypeStruct((24, D), F32),
+        compiler_params=pltpu.CompilerParams(vmem_limit_bytes=VMEM),
+        cost_estimate=pl.CostEstimate(flops=seq * 24 * D, bytes_accessed=10 ** 6, transcendentals=0),
+    )(recv, after)
+
+
+def last_kernel(recv_ref, own_ref, sq_ref, sk_ref, sv_ref, dq_in, dk_in, dv_in, after, dq_ref, dk_ref, dv_ref):
     every = recv_ref[...].astype(F32)
     count = every.shape[0] * 8
     top = every[:, :8].reshape(count, PROJ)
@@ -227,7 +266,7 @@
                              old[...].astype(F32)).astype(BF16)
 
 
-def last(recv, send, sums, grads):
+def last(recv, send, sums, grads, after):
     seq = recv.shape[0]
     tok = grads[0].shape[0]
     sub = pl.BlockSpec((tok // DIL, SUB, D), lambda i: (0, 0, 0))
@@ -237,36 +276,36 @@
         last_kernel,
         grid=(1,),
         in_specs=[pl.BlockSpec((seq, 16, PROJ), lambda i: (0, 0, 0)),
-                  pl.BlockSpec((1, 16, PROJ), lambda i: (0, 0, 0))] + [sel] * 3 + [sub] * 3,
+                  pl.BlockSpec((1, 16, PROJ), lambda i: (0, 0, 0))] + [sel] * 3 + [sub] * 3
+        + [pl.BlockSpec(memory_space=pl.ANY)],
         out_specs=[sub] * 3,
         out_shape=[view] * 3,
         input_output_aliases={5: 0, 6: 1, 7: 2},
         compiler_params=pltpu.CompilerParams(vmem_limit_bytes=VMEM),
         cost_estimate=pl.CostEstimate(flops=7 * 2 * 96 * 256 * D, bytes_accessed=4 * 10 ** 6,
                                       transcendentals=2 * 96 * 256),
-    )(recv, send, *sums, *[x.reshape(view.shape) for x in grads])
+    )(recv, send, *sums, *[x.reshape(view.shape) for x in grads], after)
 
 
 def on_device(queries, key_rows, value_rows, saved_out, logsumexp, out_grad, proj_weight):
     q, k, v = queries[0], key_rows[0], value_rows[0]
-    lse = logsumexp[0]
+    lse = jnp.transpose(logsumexp, (1, 0, 2))
     tok = q.shape[0]
     seq = lax.axis_size("seq")
     rep = lax.axis_size("rep")
     attn, delta, send = front(saved_out[0], out_grad[0], proj_weight, lse, q, k, v, seq)
     recv = lax.all_to_all(send, "seq", 0, 0)
-    *grads, sq, sk, sv = local_level(q, k, v, attn, lse, delta)
-    total = jnp.sum(recv[:, :, PROJ:].astype(F32), axis=0)
-    rest = total[:, D:]
-    mine = jnp.concatenate([total[:, :D], jnp.concatenate([rest[:8], rest[8:]], axis=1)], axis=0)
+    part = local_level(0, 5, q, k, v, attn, lse, delta)
+    mine = sum_terms(recv, part[3])
 
     def other(x, bit):
         return lax.ppermute(x, "rep", [(i, i ^ bit) for i in range(rep)])
 
-    pair_sum = mine + other(mine, 2)
+    part = local_level(5, 1, q, k, v, attn, lse, delta, before=part, after=mine)
+    pair_sum = add_after(mine, other(mine, 2), part[3])
+    outs = last(recv, send, part[3:], part[:3], after=pair_sum)
     all_sum = pair_sum + other(pair_sum, 1)
     projection_gradient = all_sum * (1.0 / math.sqrt(rep * seq * tok))
-    outs = last(recv, send, (sq, sk, sv), grads)
     return (*[x.reshape(1, tok, D) for x in outs], projection_gradient)
 
 

time: 104 us -> 79.7 us (0.77)
  the two profiles are of different devices: /device:TPU:1 before, /device:TPU:11 now
where the time goes in v2:
time: 79.7 us; the launch traced here: 79.3 us
  Pallas kernels  53.2 us (67%)
  starting transfers between devices  13.2 us (17%)
  waiting for transfers between devices  11 us (14%)
    pallas_call x2, Pallas kernels, local_level(): pl.pallas_call(functools.partial(local_kernel, 256, first), grid=(count,)...  36.2 us
    all_to_all x1, waiting for transfers between devices, on_device(): recv = lax.all_to_all(send, 'seq', 0, 0)  11 us
    pallas_call x1, Pallas kernels, front(): pl.pallas_call(functools.partial(front_kernel, steps, seq), grid=(steps,)...  9.84 us
    all_to_all x1, starting transfers between devices, on_device(): recv = lax.all_to_all(send, 'seq', 0, 0)  8.86 us
    ppermute x2, starting transfers between devices, other(): return lax.ppermute(x, 'rep', [(i, i ^ bit) for i in range(rep)])  4.31 us
    pallas_call x1, Pallas kernels, last(): pl.pallas_call(last_kernel, grid=(1,), in_specs=[pl.BlockSpec((seq, 16, P...  3.55 us
    pallas_call x1, Pallas kernels, sum_terms(): pl.pallas_call(terms_kernel, grid=(1,), in_specs=[pl.BlockSpec((pl.Elemen...  2.07 us
  transfers between devices with their start and end apart: 3, of which 1 were waited for; matrix products, arithmetic and copies ran while one was open for 0% of the time, Pallas kernels for 50%

profile of v2, /device:TPU:11, one launch (start us, length us, event | category | flops | bytes accessed | tf_op | source)
XLA Modules:
  0.0 79.3 jit_solution(2726913067226775230)
XLA Ops:
  0.6 9.8 %shard_map.102 = (bf16[1024,768]{1,0:T(8,128)(2,1)}, f32[16,1024]{1,0:T(8,128)}, bf16[32,16,2816]{2,1,0:T(8,128)(2,1)}) custom-call(bf16[1024,768]{1,0:T(8,128)(2,1)} %bitcast.30, bf16[1024,768]{1,0:T(8,128)(2,1)} %bitcast.31, bf16[768,768]{1,0:T(8,128)(2,1)} %w_ref.1, f32[12,1,1024]{2,1,0:T(1,128)} %bitcast.32, bf16[8,128,768]{2,1,0:T(8,128)(2,1)} %bitcast.15, ...), custom_call_target="tpu_custom_call" | custom-call | flops 2415919104 | bytes 9000000 | tf_op jit(solution)/shard_map/pallas_call | solution.py:110
  10.5 8.9 %all-to-all-start = ((bf16[32,16,2816]{2,1,0:T(8,128)(2,1)}), bf16[32,16,2816]{2,1,0:T(8,128)(2,1)}, u32[]{:S(2)}, u32[]{:S(2)}) async-start(bf16[32,16,2816]{2,1,0:T(8,128)(2,1)} %get-tuple-element.22.own_ref), calls=%async_computation | async-start | bytes 5767168 | tf_op jit(solution)/shard_map/all_to_all | solution.py:297
  19.3 28.9 %shard_map.103 = (bf16[1024,768]{1,0:T(8,128)(2,1)}, bf16[1024,768]{1,0:T(8,128)(2,1)}, bf16[1024,768]{1,0:T(8,128)(2,1)}, f32[8,768]{1,0:T(8,128)}, f32[8,768]{1,0:T(8,128)}, /*index=5*/f32[8,768]{1,0:T(8,128)}) custom-call(bf16[1024,768]{1,0:T(8,128)(2,1)} %bitcast.16, bf16[1024,768]{1,0:T(8,128)(2,1)} %bitcast.19, bf16[1024,768]{1,0:T(8,128)(2,1)} %bitcast.22, ...), custom_call_target="tpu_custom_call" | custom-call | flops 13421772800 | bytes 10000000 | tf_op jit(solution)/shard_map/pallas_call | solution.py:172
  48.2 11.0 %all-to-all-done.recv_ref = bf16[32,16,2816]{2,1,0:T(8,128)(2,1)} async-done(((bf16[32,16,2816]{2,1,0:T(8,128)(2,1)}), bf16[32,16,2816]{2,1,0:T(8,128)(2,1)}, u32[]{:S(2)}, u32[]{:S(2)}) %all-to-all-start) | async-done | bytes 2883616 | tf_op jit(solution)/shard_map/all_to_all | solution.py:297
  59.2 2.1 %shard_map.104.rest_6_.a_ref = f32[24,768]{1,0:T(8,128)} custom-call(bf16[32,16,2816]{2,1,0:T(8,128)(2,1)} %all-to-all-done.recv_ref, f32[8,768]{1,0:T(8,128)} %get-tuple-element.28.after.rest_3_), custom_call_target="tpu_custom_call" | custom-call | flops 589824 | bytes 1000000 | tf_op jit(solution)/shard_map/pallas_call | solution.py:212
  61.3 2.0 %collective-permute-start = (f32[24,768]{1,0:T(8,128)}, f32[24,768]{1,0:T(8,128)S(1)}, u32[]{:S(2)}, u32[]{:S(2)}) collective-permute-start(f32[24,768]{1,0:T(8,128)} %shard_map.104.rest_6_.a_ref), channel_id=1, source_target_pairs={{0,2},{1,3},{2,0},{3,1},{4,6},{5,7},{6,4},{7,5},{8,10},{9,11},{10,... | collective-permute-start | bytes 221192 | tf_op jit(solution)/shard_map/ppermute | solution.py:302
  63.3 7.3 %shard_map.105 = (bf16[1024,768]{1,0:T(8,128)(2,1)}, bf16[1024,768]{1,0:T(8,128)(2,1)}, bf16[1024,768]{1,0:T(8,128)(2,1)}, f32[8,768]{1,0:T(8,128)}, f32[8,768]{1,0:T(8,128)}, /*index=5*/f32[8,768]{1,0:T(8,128)}) custom-call(bf16[1024,768]{1,0:T(8,128)(2,1)} %bitcast.17, ...), custom_call_target="tpu_custom_call", output_to_operand_aliasing={{0}: (6, {}), {1}: (7, {}), {2}: (8, {}), {3}: (9, {}), {4}... | custom-call | flops 2684354560 | bytes 2000000 | tf_op jit(solution)/shard_map/pallas_call | solution.py:172
  70.6 0.0 collective-permute-done.b_ref
  70.6 0.0 copy-start.1
  70.6 0.6 copy-done.1
  71.3 1.6 %shard_map.106.after = f32[24,768]{1,0:T(8,128)} custom-call(f32[24,768]{1,0:T(8,128)} %shard_map.104.rest_6_.a_ref, f32[24,768]{1,0:T(8,128)} %copy-done.1, f32[8,768]{1,0:T(8,128)} %get-tuple-element.31.after.sq_ref), custom_call_target="tpu_custom_call" | custom-call | flops 18432 | bytes 221184 | tf_op jit(solution)/shard_map/pallas_call | solution.py:194
  72.8 2.3 %collective-permute-start.1 = (f32[24,768]{1,0:T(8,128)}, f32[24,768]{1,0:T(8,128)S(1)}, u32[]{:S(2)}, u32[]{:S(2)}) collective-permute-start(f32[24,768]{1,0:T(8,128)} %shard_map.106.after), channel_id=1, source_target_pairs={{0,1},{1,0},{2,3},{3,2},{4,5},{5,4},{6,7},{7,6},{8,9},{9,8},{10,11... | collective-permute-start | bytes 221192 | tf_op jit(solution)/shard_map/ppermute | solution.py:302
  75.1 0.0 copy-start
  75.1 3.5 %shard_map.107 = (bf16[8,128,768]{2,1,0:T(8,128)(2,1)}, bf16[8,128,768]{2,1,0:T(8,128)(2,1)}, bf16[8,128,768]{2,1,0:T(8,128)(2,1)}) custom-call(bf16[32,16,2816]{2,1,0:T(8,128)(2,1)} %all-to-all-done.recv_ref, bf16[32,16,2816]{2,1,0:T(8,128)(2,1)} %get-tuple-element.22.own_ref, ...), custom_call_target="tpu_custom_call", output_to_operand_aliasing={{0}: (5, {}), {1}: (6, {}), {2}: (7, {})} | custom-call | flops 264241152 | bytes 4000000 | tf_op jit(solution)/shard_map/pallas_call | solution.py:275
  78.7 0.0 collective-permute-done.1
  78.7 0.0 copy-done
  78.7 0.6 add_multiply_fusion
Async XLA Ops:
  10.5 48.8 %all-to-all-start = ((bf16[32,16,2816]{2,1,0:T(8,128)(2,1)}), bf16[32,16,2816]{2,1,0:T(8,128)(2,1)}, u32[]{:S(2)}, u32[]{:S(2)}) async-start(bf16[32,16,2816]{2,1,0:T(8,128)(2,1)} %get-tuple-element.22.own_ref), calls=%async_computation | async-start | bytes 5767168 | tf_op jit(solution)/shard_map/all_to_all | solution.py:297
  61.3 9.3 %collective-permute-start = (f32[24,768]{1,0:T(8,128)}, f32[24,768]{1,0:T(8,128)S(1)}, u32[]{:S(2)}, u32[]{:S(2)}) collective-permute-start(f32[24,768]{1,0:T(8,128)} %shard_map.104.rest_6_.a_ref), channel_id=1, source_target_pairs={{0,2},{1,3},{2,0},{3,1},{4,6},{5,7},{6,4},{7,5},{8,10},{9,11},{10,... | collective-permute-start | bytes 221192 | tf_op jit(solution)/shard_map/ppermute | solution.py:302
  70.6 0.6 copy-start.1
  72.8 5.8 %collective-permute-start.1 = (f32[24,768]{1,0:T(8,128)}, f32[24,768]{1,0:T(8,128)S(1)}, u32[]{:S(2)}, u32[]{:S(2)}) collective-permute-start(f32[24,768]{1,0:T(8,128)} %shard_map.106.after), channel_id=1, source_target_pairs={{0,1},{1,0},{2,3},{3,2},{4,5},{5,4},{6,7},{7,6},{8,9},{9,8},{10,11... | collective-permute-start | bytes 221192 | tf_op jit(solution)/shard_map/ppermute | solution.py:302
  75.1 3.6 %copy-start = (f32[24,768]{1,0:T(8,128)S(1)}, f32[24,768]{1,0:T(8,128)}, u32[]{:S(2)}) copy-start(f32[24,768]{1,0:T(8,128)} %shard_map.106.after) | copy-start | bytes 221188

commit v3 on v2

--- a/solution.py
+++ b/solution.py
@@ -17,9 +17,12 @@
 SUB = 16
 LOG2E = math.log2(math.e)
 SCALE = HW ** -0.5
-STAT = 2 * D
+HALF = D // 2
+PART = HEADS // 2
+STAT = 2 * HALF
 PROJ = STAT + 128
 TERM = D + D // 2
+MATE = 4
 VMEM = 62 * 2 ** 20
 
 
@@ -36,8 +39,8 @@
     return jnp.sum(jnp.where(keep, rows.astype(F32), 0.0), axis=1)
 
 
-def three_terms(x):
-    x = jnp.where(iota(x.shape, 1) < HEADS, x, 0.0)
+def three_terms(x, half):
+    x = jnp.where(iota(x.shape, 1) < PART, pltpu.roll(x, 128 - PART, 1) if half else x, 0.0)
     hi = x.astype(BF16).astype(F32)
     mid = (x - hi).astype(BF16).astype(F32)
     low = ((x - hi) - mid).astype(BF16).astype(F32)
@@ -88,12 +91,16 @@
         lse = jnp.concatenate(
             [sum(jnp.where(lane == h, lse_ref[h, :, DIL * j:DIL * (j + 1)], 0.0) for h in range(HEADS))
              for j in range(8)], axis=0)
-        top = jnp.concatenate([head_rows(q_ref[...]), head_rows(k_ref[...]), three_terms(lse)], axis=1)
-        bot = jnp.concatenate([head_rows(v_ref[...]), gsel[...], three_terms(dsel[...])], axis=1)
-        own = jnp.concatenate([top, bot], axis=0).astype(BF16)
+        rows = [head_rows(q_ref[...]), head_rows(k_ref[...]), head_rows(v_ref[...]), gsel[...]]
+        own = []
+        for half in range(2):
+            q, k, v, g = (x[:, HALF * half:HALF * (half + 1)] for x in rows)
+            top = jnp.concatenate([q, k, three_terms(lse, half)], axis=1)
+            bot = jnp.concatenate([v, g, three_terms(dsel[...], half)], axis=1)
+            own.append(jnp.concatenate([top, bot], axis=0).astype(BF16))
         share = D // seq
         for s in range(seq):
-            send_ref[s, :, 0:PROJ] = own
+            send_ref[s, :, 0:PROJ] = own[1 if s & MATE else 0]
             send_ref[s, :, PROJ:PROJ + D] = acc[share * s:share * s + 16].astype(BF16)
             rest = acc[share * s + 16:share * s + 24]
             send_ref[s, :, PROJ + D:] = jnp.concatenate(
@@ -185,106 +192,110 @@
     )(q, k, v, g, lse, delta, *extra)
 
 
-def add_kernel(a_ref, b_ref, after, out_ref):
-    out_ref[...] = a_ref[...] + b_ref[...]
-
-
-def add_after(a, b, after):
-    whole = pl.BlockSpec(a.shape, lambda: (0, 0))
-    return pl.pallas_call(
-        add_kernel,
-        in_specs=[whole, whole, pl.BlockSpec(memory_space=pl.ANY)],
-        out_specs=whole,
-        out_shape=jax.ShapeDtypeStruct(a.shape, a.dtype),
-        cost_estimate=pl.CostEstimate(flops=a.size, bytes_accessed=12 * a.size, transcendentals=0),
-    )(a, b, after)
-
-
-def terms_kernel(recv_ref, after, out_ref):
-    total = jnp.sum(recv_ref[...].astype(F32), axis=0)
-    out_ref[:16] = total[:, :D]
-    out_ref[16:, :D // 2] = total[:8, D:]
-    out_ref[16:, D // 2:] = total[8:, D:]
-
-
-def sum_terms(recv, after):
-    seq = recv.shape[0]
-    return pl.pallas_call(
-        terms_kernel,
-        grid=(1,),
-        in_specs=[pl.BlockSpec((pl.Element(seq), pl.Element(16), pl.Element(TERM)), lambda i: (0, 0, PROJ)),
-                  pl.BlockSpec(memory_space=pl.ANY)],
-        out_specs=pl.BlockSpec((24, D), lambda i: (0, 0)),
-        out_shape=jax.ShapeDtypeStruct((24, D), F32),
-        compiler_params=pltpu.CompilerParams(vmem_limit_bytes=VMEM),
-        cost_estimate=pl.CostEstimate(flops=seq * 24 * D, bytes_accessed=10 ** 6, transcendentals=0),
-    )(recv, after)
-
-
-def last_kernel(recv_ref, own_ref, sq_ref, sk_ref, sv_ref, dq_in, dk_in, dv_in, after, dq_ref, dk_ref, dv_ref):
-    every = recv_ref[...].astype(F32)
+def dilated_kernel(place, recv_ref, own_ref, mate_ref, after, sum_ref, mine_ref, theirs_ref):
+    total = jnp.sum(recv_ref[:, :, PROJ:].astype(F32), axis=0)
+    sum_ref[:16] = total[:, :D]
+    sum_ref[16:, :D // 2] = total[:8, D:]
+    sum_ref[16:, D // 2:] = total[8:, D:]
+    every = recv_ref[:, :, :PROJ].astype(F32)
     count = every.shape[0] * 8
     top = every[:, :8].reshape(count, PROJ)
     bot = every[:, 8:].reshape(count, PROJ)
-    q, k = top[:, :D].astype(BF16), top[:, D:2 * D].astype(BF16)
-    v, g = bot[:, :D].astype(BF16), bot[:, D:2 * D].astype(BF16)
-    lse = join_terms(top[:, STAT:]).T[:HEADS]
-    delta = join_terms(bot[:, STAT:]).T[:HEADS]
-    own = own_ref[0].astype(F32)
-    own_head = iota((HEADS, 8, D), 0) == iota((HEADS, 8, D), 2) // HW
+    q, k = top[:, :HALF].astype(BF16), top[:, HALF:STAT].astype(BF16)
+    v, g = bot[:, :HALF].astype(BF16), bot[:, HALF:STAT].astype(BF16)
+    lse = join_terms(top[:, STAT:]).T[:PART]
+    delta = join_terms(bot[:, STAT:]).T[:PART]
+    own, mate = own_ref[0].astype(F32), mate_ref[0].astype(F32)
+    top = jnp.concatenate([own[:8], mate[:8]], axis=0)
+    bot = jnp.concatenate([own[8:], mate[8:]], axis=0)
+    own_head = iota((PART, 16, HALF), 0) == iota((PART, 16, HALF), 2) // HW
 
     def by_head(x):
-        return jnp.where(own_head, jnp.broadcast_to(x[None], (HEADS, 8, D)), 0.0).reshape(HEADS * 8, D).astype(BF16)
+        return jnp.where(own_head, jnp.broadcast_to(x[None], own_head.shape), 0.0).reshape(PART * 16, HALF).astype(BF16)
 
     def column(x):
-        x = jnp.broadcast_to(join_terms(x)[None], (HEADS, 8, 128))
+        x = jnp.broadcast_to(join_terms(x)[None], (PART, 16, 128))
         x = jnp.where(iota(x.shape, 0) == iota(x.shape, 2), x, 0.0)
-        return jnp.sum(x.reshape(HEADS * 8, 128), axis=1, keepdims=True)
+        return jnp.sum(x.reshape(PART * 16, 128), axis=1, keepdims=True)
 
     def row(x):
-        return jnp.broadcast_to(x[:, None], (HEADS, 8, count)).reshape(HEADS * 8, count)
+        return jnp.broadcast_to(x[:, None], (PART, 16, count)).reshape(PART * 16, count)
 
     def back(x):
-        return jnp.sum(jnp.where(own_head, x.reshape(HEADS, 8, D), 0.0), axis=0)
+        return jnp.sum(jnp.where(own_head, x.reshape(PART, 16, HALF), 0.0), axis=0)
 
     def pieces(left_s, right_s, left_p, right_p, lse, delta):
         prob = jnp.exp2(dot(left_s, right_s, 1, 1) * (SCALE * LOG2E) - lse * LOG2E)
         dscore = (prob * (dot(left_p, right_p, 1, 1) - delta)).astype(BF16)
         return prob.astype(BF16), dscore
 
-    _, dscore = pieces(by_head(own[:8, :D]), k, by_head(own[8:, D:2 * D]), v,
-                       column(own[:8, STAT:]), column(own[8:, STAT:]))
+    _, dscore = pieces(by_head(top[:, :HALF]), k, by_head(bot[:, HALF:STAT]), v,
+                       column(top[:, STAT:]), column(bot[:, STAT:]))
     grad_q = back(dot(dscore, k, 1, 0)) * SCALE
-    weight, dscore = pieces(by_head(own[:8, D:2 * D]), q, by_head(own[8:, :D]), g, row(lse), row(delta))
+    weight, dscore = pieces(by_head(top[:, HALF:STAT]), q, by_head(bot[:, :HALF]), g, row(lse), row(delta))
     grad_k = back(dot(dscore, q, 1, 0)) * SCALE
     grad_v = back(dot(weight, g, 1, 0))
+    for i, grad in enumerate((grad_q, grad_k, grad_v)):
+        mine_ref[:, HALF * i:HALF * (i + 1)] = grad[:8]
+        theirs_ref[:, HALF * i:HALF * (i + 1)] = grad[8:]
+
+
+def dilated_level(recv, me, after):
+    seq, _, width = recv.shape
+    place = jnp.stack([me, me ^ MATE]).astype(jnp.int32)
+    whole = pl.BlockSpec((8, 3 * HALF), lambda i, p: (0, 0))
+    return pl.pallas_call(
+        dilated_kernel,
+        grid_spec=pltpu.PrefetchScalarGridSpec(
+            num_scalar_prefetch=1,
+            grid=(1,),
+            in_specs=[pl.BlockSpec((seq, 16, width), lambda i, p: (0, 0, 0)),
+                      pl.BlockSpec((1, 16, PROJ), lambda i, p: (p[0], 0, 0)),
+                      pl.BlockSpec((1, 16, PROJ), lambda i, p: (p[1], 0, 0)),
+                      pl.BlockSpec(memory_space=pl.ANY)],
+            out_specs=[pl.BlockSpec((24, D), lambda i, p: (0, 0)), whole, whole]),
+        out_shape=[jax.ShapeDtypeStruct((24, D), F32)] + [jax.ShapeDtypeStruct((8, 3 * HALF), F32)] * 2,
+        compiler_params=pltpu.CompilerParams(vmem_limit_bytes=VMEM),
+        cost_estimate=pl.CostEstimate(flops=7 * 2 * 96 * 256 * HALF, bytes_accessed=3 * 10 ** 6,
+                                      transcendentals=2 * 96 * 256),
+    )(place, recv, recv, recv, after)
+
+
+def last_kernel(scale, place, mine_ref, theirs_ref, sq_ref, sk_ref, sv_ref, a_ref, b_ref, c_ref, d_ref,
+                dq_in, dk_in, dv_in, dq_ref, dk_ref, dv_ref, proj_ref):
+    proj_ref[...] = ((a_ref[...] + b_ref[...]) + (c_ref[...] + d_ref[...])) * scale
+    first = place[0] == 0
     here = iota((8, SUB, D), 1) == iota((8, SUB, D), 2) // HW
-    for sel, grad, old, out in ((sq_ref, grad_q, dq_in, dq_ref), (sk_ref, grad_k, dk_in, dk_ref),
-                                (sv_ref, grad_v, dv_in, dv_ref)):
-        total = sel[...] + grad
+    for i, (sel, old, out) in enumerate(((sq_ref, dq_in, dq_ref), (sk_ref, dk_in, dk_ref), (sv_ref, dv_in, dv_ref))):
+        part = slice(HALF * i, HALF * (i + 1))
+        mine, theirs = mine_ref[:, part], theirs_ref[:, part]
+        total = sel[...] + jnp.concatenate([jnp.where(first, mine, theirs), jnp.where(first, theirs, mine)], axis=1)
         out[...] = jnp.where(here, jnp.broadcast_to(total[:, None], (8, SUB, D)),
                              old[...].astype(F32)).astype(BF16)
 
 
-def last(recv, send, sums, grads, after):
-    seq = recv.shape[0]
+def last(me, mine, theirs, sums, terms, grads, scale):
     tok = grads[0].shape[0]
-    sub = pl.BlockSpec((tok // DIL, SUB, D), lambda i: (0, 0, 0))
-    sel = pl.BlockSpec((tok // DIL, D), lambda i: (0, 0))
+    place = jnp.reshape(me & MATE, (1,)).astype(jnp.int32)
+    sub = pl.BlockSpec((tok // DIL, SUB, D), lambda i, p: (0, 0, 0))
+
+    def whole(x):
+        return pl.BlockSpec(x.shape, lambda i, p: (0, 0))
+
     view = jax.ShapeDtypeStruct((tok // DIL, DIL, D), BF16)
+    small = (mine, theirs, *sums, *terms)
     return pl.pallas_call(
-        last_kernel,
-        grid=(1,),
-        in_specs=[pl.BlockSpec((seq, 16, PROJ), lambda i: (0, 0, 0)),
-                  pl.BlockSpec((1, 16, PROJ), lambda i: (0, 0, 0))] + [sel] * 3 + [sub] * 3
-        + [pl.BlockSpec(memory_space=pl.ANY)],
-        out_specs=[sub] * 3,
-        out_shape=[view] * 3,
-        input_output_aliases={5: 0, 6: 1, 7: 2},
-        compiler_params=pltpu.CompilerParams(vmem_limit_bytes=VMEM),
-        cost_estimate=pl.CostEstimate(flops=7 * 2 * 96 * 256 * D, bytes_accessed=4 * 10 ** 6,
-                                      transcendentals=2 * 96 * 256),
-    )(recv, send, *sums, *[x.reshape(view.shape) for x in grads], after)
+        functools.partial(last_kernel, scale),
+        grid_spec=pltpu.PrefetchScalarGridSpec(
+            num_scalar_prefetch=1,
+            grid=(1,),
+            in_specs=[whole(x) for x in small] + [sub] * 3,
+            out_specs=[sub] * 3 + [whole(terms[0])]),
+        out_shape=[view] * 3 + [jax.ShapeDtypeStruct(terms[0].shape, F32)],
+        input_output_aliases={1 + len(small) + i: i for i in range(3)},
+        compiler_params=pltpu.CompilerParams(vmem_limit_bytes=16 * 2 ** 20),
+        cost_estimate=pl.CostEstimate(flops=10 ** 6, bytes_accessed=2 * 10 ** 6, transcendentals=0),
+    )(place, *small, *[x.reshape(view.shape) for x in grads])
 
 
 def on_device(queries, key_rows, value_rows, saved_out, logsumexp, out_grad, proj_weight):
@@ -295,17 +306,17 @@
     rep = lax.axis_size("rep")
     attn, delta, send = front(saved_out[0], out_grad[0], proj_weight, lse, q, k, v, seq)
     recv = lax.all_to_all(send, "seq", 0, 0)
-    part = local_level(0, 5, q, k, v, attn, lse, delta)
-    mine = sum_terms(recv, part[3])
-
-    def other(x, bit):
-        return lax.ppermute(x, "rep", [(i, i ^ bit) for i in range(rep)])
-
-    part = local_level(5, 1, q, k, v, attn, lse, delta, before=part, after=mine)
-    pair_sum = add_after(mine, other(mine, 2), part[3])
-    outs = last(recv, send, part[3:], part[:3], after=pair_sum)
-    all_sum = pair_sum + other(pair_sum, 1)
-    projection_gradient = all_sum * (1.0 / math.sqrt(rep * seq * tok))
+    me = lax.axis_index("seq")
+    part = local_level(0, 4, q, k, v, attn, lse, delta)
+    term, mine, theirs = dilated_level(recv, me, part[3])
+
+    def other(x, axis, size, bit):
+        return lax.ppermute(x, axis, [(i, i ^ bit) for i in range(size)])
+
+    theirs = other(theirs, "seq", seq, MATE)
+    terms = (term, *[other(term, "rep", rep, bit) for bit in (2, 1, 3)])
+    part = local_level(4, 2, q, k, v, attn, lse, delta, before=part, after=term)
+    *outs, projection_gradient = last(me, mine, theirs, part[3:], terms, part[:3], 1.0 / math.sqrt(rep * seq * tok))
     return (*[x.reshape(1, tok, D) for x in outs], projection_gradient)
 
 

time: 79.7 us -> 75.8 us (0.951)
  the two profiles are of different devices: /device:TPU:11 before, /device:TPU:2 now
where the time goes in v3:
time: 75.8 us; the launch traced here: 75.3 us
  Pallas kernels  51.8 us (68%)
  starting transfers between devices  14.9 us (20%)
  waiting for transfers between devices  5.04 us (7%)
  local copies, waits for them, and re-layouts  2.21 us (3%)
    pallas_call x2, Pallas kernels, local_level(): pl.pallas_call(functools.partial(local_kernel, 256, first), grid=(count,)...  36.3 us
    pallas_call x1, Pallas kernels, front(): pl.pallas_call(functools.partial(front_kernel, steps, seq), grid=(steps,)...  9.58 us
    all_to_all x1, starting transfers between devices, on_device(): recv = lax.all_to_all(send, 'seq', 0, 0)  9.54 us
    ppermute x4, starting transfers between devices, other(): return lax.ppermute(x, axis, [(i, i ^ bit) for i in range(size)])  5.38 us
    all_to_all x1, waiting for transfers between devices, on_device(): recv = lax.all_to_all(send, 'seq', 0, 0)  5.03 us
    pallas_call x1, Pallas kernels, dilated_level(): pl.pallas_call(dilated_kernel, grid_spec=pltpu.PrefetchScalarGridSpec(num...  3.83 us
    unnamed x10, local copies, waits for them, and re-layouts  2.21 us
    pallas_call x1, Pallas kernels, last(): pl.pallas_call(functools.partial(last_kernel, scale), grid_spec=pltpu.Pre...  2.07 us
  transfers between devices with their start and end apart: 5, of which 1 were waited for; matrix products, arithmetic and copies ran while one was open for 1% of the time, Pallas kernels for 48%

profile of v3, /device:TPU:2, one launch (start us, length us, event | category | flops | bytes accessed | tf_op | source)
XLA Modules:
  0.0 75.3 jit_solution(9623313470618181967)
XLA Ops:
  0.6 9.6 %shard_map.102 = (bf16[1024,768]{1,0:T(8,128)(2,1)}, f32[16,1024]{1,0:T(8,128)}, bf16[32,16,2048]{2,1,0:T(8,128)(2,1)}) custom-call(bf16[1024,768]{1,0:T(8,128)(2,1)} %bitcast.24, bf16[1024,768]{1,0:T(8,128)(2,1)} %bitcast.25, bf16[768,768]{1,0:T(8,128)(2,1)} %w_ref.1, f32[12,1,1024]{2,1,0:T(1,128)} %bitcast.35, bf16[8,128,768]{2,1,0:T(8,128)(2,1)} %bitcast.26, ...), custom_call_target="tpu_custom_call" | custom-call | flops 2415919104 | bytes 9000000 | tf_op jit(solution)/shard_map/pallas_call | solution.py:117
  10.2 9.5 %all-to-all-start = ((bf16[32,16,2048]{2,1,0:T(8,128)(2,1)}), bf16[32,16,2048]{2,1,0:T(8,128)(2,1)}, u32[]{:S(2)}, u32[]{:S(2)}) async-start(bf16[32,16,2048]{2,1,0:T(8,128)(2,1)} %get-tuple-element.26), calls=%async_computation | async-start | bytes 4194304 | tf_op jit(solution)/shard_map/all_to_all | solution.py:308
  19.8 0.7 pad_add_fusion.place
  20.4 23.5 %shard_map.103 = (bf16[1024,768]{1,0:T(8,128)(2,1)}, bf16[1024,768]{1,0:T(8,128)(2,1)}, bf16[1024,768]{1,0:T(8,128)(2,1)}, f32[8,768]{1,0:T(8,128)}, f32[8,768]{1,0:T(8,128)}, /*index=5*/f32[8,768]{1,0:T(8,128)}) custom-call(bf16[1024,768]{1,0:T(8,128)(2,1)} %bitcast.27, bf16[1024,768]{1,0:T(8,128)(2,1)} %bitcast.30, bf16[1024,768]{1,0:T(8,128)(2,1)} %bitcast.33, ...), custom_call_target="tpu_custom_call" | custom-call | flops 10737418240 | bytes 8000000 | tf_op jit(solution)/shard_map/pallas_call | solution.py:179
  43.9 5.0 %all-to-all-done.recv_ref.own_ref.mate_ref = bf16[32,16,2048]{2,1,0:T(8,128)(2,1)} async-done(((bf16[32,16,2048]{2,1,0:T(8,128)(2,1)}), bf16[32,16,2048]{2,1,0:T(8,128)(2,1)}, u32[]{:S(2)}, u32[]{:S(2)}) %all-to-all-start) | async-done | bytes 2097184 | tf_op jit(solution)/shard_map/all_to_all | solution.py:308
  49.0 3.8 %shard_map.104 = (f32[24,768]{1,0:T(8,128)}, f32[8,1152]{1,0:T(8,128)}, f32[8,1152]{1,0:T(8,128)}) custom-call(s32[2]{0:T(128)} %pad_add_fusion.place, bf16[32,16,2048]{2,1,0:T(8,128)(2,1)} %all-to-all-done.recv_ref.own_ref.mate_ref, bf16[32,16,2048]{2,1,0:T(8,128)(2,1)} %all-to-all-done.recv_ref.own_ref.mate_ref, ...), custom_call_target="tpu_custom_call" | custom-call | flops 132120576 | bytes 3000000 | tf_op jit(solution)/shard_map/pallas_call | solution.py:247
  52.8 0.9 %collective-permute-start.3 = (f32[24,768]{1,0:T(8,128)}, f32[24,768]{1,0:T(8,128)S(1)}, u32[]{:S(2)}, u32[]{:S(2)}) collective-permute-start(f32[24,768]{1,0:T(8,128)} %get-tuple-element.37.rest_6_.a_ref), channel_id=1, source_target_pairs={{0,3},{1,2},{2,1},{3,0},{4,7},{5,6},{6,5},{7,4},{8,11},{9,10},{10,... | collective-permute-start | bytes 221192 | tf_op jit(solution)/shard_map/ppermute | solution.py:314
  53.7 2.1 %collective-permute-start.2 = (f32[24,768]{1,0:T(8,128)}, f32[24,768]{1,0:T(8,128)S(1)}, u32[]{:S(2)}, u32[]{:S(2)}) collective-permute-start(f32[24,768]{1,0:T(8,128)} %get-tuple-element.37.rest_6_.a_ref), channel_id=1, source_target_pairs={{0,1},{1,0},{2,3},{3,2},{4,5},{5,4},{6,7},{7,6},{8,9},{9,8},{10,11... | collective-permute-start | bytes 221192 | tf_op jit(solution)/shard_map/ppermute | solution.py:314
  55.8 0.6 collective-permute-start.1
  56.4 1.7 %collective-permute-start = (f32[8,1152]{1,0:T(8,128)}, f32[8,1152]{1,0:T(8,128)S(1)}, u32[]{:S(2)}, u32[]{:S(2)}) collective-permute-start(f32[8,1152]{1,0:T(8,128)} %get-tuple-element.31), channel_id=1, source_target_pairs={{0,16},{4,20},{8,24},{12,28},{16,0},{20,4},{24,8},{28,12},{32,48},... | collective-permute-start | bytes 110600 | tf_op jit(solution)/shard_map/ppermute | solution.py:314
  58.2 0.0 copy-start.1
  58.2 0.0 copy-start.2
  58.2 12.8 %shard_map.105 = (bf16[1024,768]{1,0:T(8,128)(2,1)}, bf16[1024,768]{1,0:T(8,128)(2,1)}, bf16[1024,768]{1,0:T(8,128)(2,1)}, f32[8,768]{1,0:T(8,128)}, f32[8,768]{1,0:T(8,128)}, /*index=5*/f32[8,768]{1,0:T(8,128)}) custom-call(bf16[1024,768]{1,0:T(8,128)(2,1)} %bitcast.28, ...), custom_call_target="tpu_custom_call", output_to_operand_aliasing={{0}: (6, {}), {1}: (7, {}), {2}: (8, {}), {3}: (9, {}), {4}... | custom-call | flops 5368709120 | bytes 4000000 | tf_op jit(solution)/shard_map/pallas_call | solution.py:179
  70.9 0.0 collective-permute-done.theirs_ref
  71.0 0.0 collective-permute-done.3.d_ref
  71.0 0.0 collective-permute-done.2.c_ref
  71.0 0.0 collective-permute-done.1.b_ref
  71.0 0.0 copy-done.1
  71.0 0.0 copy-done.2
  71.0 0.0 copy-start
  71.0 0.7 copy-done
  71.7 0.7 copy-done.3
  72.5 0.7 copy-done.4
  73.2 2.1 %shard_map.106 = (bf16[8,128,768]{2,1,0:T(8,128)(2,1)}, bf16[8,128,768]{2,1,0:T(8,128)(2,1)}, bf16[8,128,768]{2,1,0:T(8,128)(2,1)}, f32[24,768]{1,0:T(8,128)}) custom-call(s32[1]{0:T(128)} %bitcast.place, f32[8,1152]{1,0:T(8,128)S(1)} %copy-done.2, ...), custom_call_target="tpu_custom_call", output_to_operand_aliasing={{0}: (10, {}), {1}: (11, {}), {2}: (12, {})} | custom-call | flops 1000000 | bytes 2000000 | tf_op jit(solution)/shard_map/pallas_call | solution.py:287
  (2 shorter events, 0.0 us)
Async XLA Ops:
  10.2 38.7 %all-to-all-start = ((bf16[32,16,2048]{2,1,0:T(8,128)(2,1)}), bf16[32,16,2048]{2,1,0:T(8,128)(2,1)}, u32[]{:S(2)}, u32[]{:S(2)}) async-start(bf16[32,16,2048]{2,1,0:T(8,128)(2,1)} %get-tuple-element.26), calls=%async_computation | async-start | bytes 4194304 | tf_op jit(solution)/shard_map/all_to_all | solution.py:308
  52.8 18.2 %collective-permute-start.3 = (f32[24,768]{1,0:T(8,128)}, f32[24,768]{1,0:T(8,128)S(1)}, u32[]{:S(2)}, u32[]{:S(2)}) collective-permute-start(f32[24,768]{1,0:T(8,128)} %get-tuple-element.37.rest_6_.a_ref), channel_id=1, source_target_pairs={{0,3},{1,2},{2,1},{3,0},{4,7},{5,6},{6,5},{7,4},{8,11},{9,10},{10,... | collective-permute-start | bytes 221192 | tf_op jit(solution)/shard_map/ppermute | solution.py:314
  53.7 17.3 %collective-permute-start.2 = (f32[24,768]{1,0:T(8,128)}, f32[24,768]{1,0:T(8,128)S(1)}, u32[]{:S(2)}, u32[]{:S(2)}) collective-permute-start(f32[24,768]{1,0:T(8,128)} %get-tuple-element.37.rest_6_.a_ref), channel_id=1, source_target_pairs={{0,1},{1,0},{2,3},{3,2},{4,5},{5,4},{6,7},{7,6},{8,9},{9,8},{10,11... | collective-permute-start | bytes 221192 | tf_op jit(solution)/shard_map/ppermute | solution.py:314
  55.8 15.2 %collective-permute-start.1 = (f32[24,768]{1,0:T(8,128)}, f32[24,768]{1,0:T(8,128)S(1)}, u32[]{:S(2)}, u32[]{:S(2)}) collective-permute-start(f32[24,768]{1,0:T(8,128)} %get-tuple-element.37.rest_6_.a_ref), channel_id=1, source_target_pairs={{0,2},{1,3},{2,0},{3,1},{4,6},{5,7},{6,4},{7,5},{8,10},{9,11},{10,... | collective-permute-start | bytes 221192 | tf_op jit(solution)/shard_map/ppermute | solution.py:314
  56.4 14.5 %collective-permute-start = (f32[8,1152]{1,0:T(8,128)}, f32[8,1152]{1,0:T(8,128)S(1)}, u32[]{:S(2)}, u32[]{:S(2)}) collective-permute-start(f32[8,1152]{1,0:T(8,128)} %get-tuple-element.31), channel_id=1, source_target_pairs={{0,16},{4,20},{8,24},{12,28},{16,0},{20,4},{24,8},{28,12},{32,48},... | collective-permute-start | bytes 110600 | tf_op jit(solution)/shard_map/ppermute | solution.py:314
  58.2 12.8 %copy-start.1 = (f32[24,768]{1,0:T(8,128)S(1)}, f32[24,768]{1,0:T(8,128)}, u32[]{:S(2)}) copy-start(f32[24,768]{1,0:T(8,128)} %get-tuple-element.37.rest_6_.a_ref) | copy-start | bytes 221188
  58.2 12.8 %copy-start.2 = (f32[8,1152]{1,0:T(8,128)S(1)}, f32[8,1152]{1,0:T(8,128)}, u32[]{:S(2)}) copy-start(f32[8,1152]{1,0:T(8,128)} %get-tuple-element.30.mine_ref) | copy-start | bytes 110596
  71.0 0.7 copy-start
  71.7 0.7 copy-start.3
  72.5 0.7 copy-start.4

commit v4 on v3

v4 whole, which is shorter than its diff:
```python
import functools
import math

import jax
import jax.numpy as jnp
from jax import lax
from jax.experimental import pallas as pl
from jax.experimental.pallas import tpu as pltpu
from jax.sharding import PartitionSpec as P

F32 = jnp.float32
BF16 = jnp.bfloat16
DIL = 128
HEADS = 12
HW = 64
D = HEADS * HW
SUB = 16
LOG2E = math.log2(math.e)
SCALE = HW ** -0.5
HALF = D // 2
PART = HEADS // 2
STAT = 2 * HALF
PROJ = STAT + 128
TERM = D + D // 2
MATE = 4
VMEM = 62 * 2 ** 20


def dot(a, b, ca, cb):
    return lax.dot_general(a, b, (((ca,), (cb,)), ((), ())), preferred_element_type=F32)


def iota(shape, axis):
    return lax.broadcasted_iota(jnp.int32, shape, axis)


def head_rows(rows):
    keep = iota((1, SUB, D), 1) == iota((1, SUB, D), 2) // HW
    return jnp.sum(jnp.where(keep, rows.astype(F32), 0.0), axis=1)


def three_terms(x, half):
    x = jnp.where(iota(x.shape, 1) < PART, pltpu.roll(x, 128 - PART, 1) if half else x, 0.0)
    hi = x.astype(BF16).astype(F32)
    mid = (x - hi).astype(BF16).astype(F32)
    low = ((x - hi) - mid).astype(BF16).astype(F32)
    return hi + pltpu.roll(mid, 16, 1) + pltpu.roll(low, 32, 1)


def join_terms(x):
    return (x + pltpu.roll(x, 112, 1)) + pltpu.roll(x, 96, 1)


def front_kernel(chunks, seq, saved_hbm, grad_hbm, w_hbm, lse_ref, q_hbm, k_hbm, v_hbm,
                 attn_hbm, delta_ref, send_hbm,
                 saved_ref, grad_ref, w_ref, pick_ref, attn_ref, send_ref, acc, in_sems, out_sems):
    tok = saved_ref.shape[0]
    rows = tok // chunks
    groups = rows // DIL
    halves = [pl.ds(i * (tok // 2), tok // 2) for i in range(2)]

    loads = []

    def load(source, target):
        loads.append(pltpu.make_async_copy(source, target, in_sems.at[len(loads)]))
        loads[-1].start()

    for half in halves:
        load(grad_hbm.at[half], grad_ref.at[half])
        load(saved_hbm.at[half], saved_ref.at[half])
    load(w_hbm, w_ref)
    for i, x in enumerate((q_hbm, k_hbm, v_hbm)):
        load(x.at[:, pl.ds(0, SUB)], pick_ref.at[i])

    stores = []

    def store(source, target):
        stores.append(pltpu.make_async_copy(source, target, out_sems.at[len(stores)]))
        stores[-1].start()

    loads[0].wait()
    loads[1].wait()
    acc[...] = dot(saved_ref[halves[0]], grad_ref[halves[0]], 0, 0)
    loads[2].wait()
    loads[3].wait()
    share = D // seq
    for i in range(2):
        wide = slice(HALF * i, HALF * (i + 1))
        term = acc[wide] + dot(saved_ref[halves[1], wide], grad_ref[halves[1]], 0, 0)
        for s in range(seq // 2):
            here = send_ref.at[i * (seq // 2) + s]
            here[:, PROJ:PROJ + D] = term[share * s:share * s + 16].astype(BF16)
            rest = term[share * s + 16:share * s + 24]
            here[:, PROJ + D:] = jnp.concatenate([rest[:, :D // 2], rest[:, D // 2:]], axis=0).astype(BF16)
        some = (pl.ds(i * (seq // 2), seq // 2), slice(None), pl.ds(PROJ, TERM))
        store(send_ref.at[some], send_hbm.at[some])

    loads[4].wait()
    pick = (iota((D, 128), 0) // HW == iota((D, 128), 1)).astype(BF16)
    diag = iota((1, DIL, 128), 1) == iota((1, DIL, 128), 2)
    picked_g, picked_d = [], []
    for c in range(chunks):
        part = pl.ds(c * rows, rows)
        attn = dot(grad_ref[part], w_ref[...], 1, 1).astype(BF16)
        attn_ref[part] = attn
        store(attn_ref.at[part], attn_hbm.at[part])
        attn = attn.astype(F32)
        prod = attn * saved_ref[part].astype(F32)
        hi = prod.astype(BF16)
        low = (prod - hi.astype(F32)).astype(BF16)
        delta = dot(hi, pick, 1, 0) + dot(low, pick, 1, 0)
        delta_ref[:, part] = delta.T[:SUB]
        picked_g.append(head_rows(attn.reshape(groups, DIL, D)[:, :SUB]))
        picked_d.append(jnp.sum(jnp.where(diag, delta.reshape(groups, DIL, 128), 0.0), axis=1))

    for copy in loads[5:]:
        copy.wait()
    lane = iota((1, 128), 1)
    lse = jnp.concatenate(
        [sum(jnp.where(lane == h, lse_ref[h, :, DIL * j:DIL * (j + 1)], 0.0) for h in range(HEADS))
         for j in range(tok // DIL)], axis=0)
    delta = jnp.concatenate(picked_d, axis=0)
    picked = [head_rows(pick_ref[0]), head_rows(pick_ref[1]), head_rows(pick_ref[2]),
              jnp.concatenate(picked_g, axis=0)]
    own = []
    for half in range(2):
        q, k, v, g = (x[:, HALF * half:HALF * (half + 1)] for x in picked)
        top = jnp.concatenate([q, k, three_terms(lse, half)], axis=1)
        bot = jnp.concatenate([v, g, three_terms(delta, half)], axis=1)
        own.append(jnp.concatenate([top, bot], axis=0).astype(BF16))
    for s in range(seq):
        send_ref[s, :, 0:PROJ] = own[1 if s & MATE else 0]
    store(send_ref.at[:, :, pl.ds(0, PROJ)], send_hbm.at[:, :, pl.ds(0, PROJ)])
    for copy in stores:
        copy.wait()


def front(saved, grad, w, lse, q, k, v, seq):
    tok = saved.shape[0]
    chunks = 2
    view = lambda x: x.reshape(tok // DIL, DIL, D)
    anywhere = pl.BlockSpec(memory_space=pl.ANY)
    inside = pl.BlockSpec(memory_space=pltpu.VMEM)
    width = PROJ + TERM
    return pl.pallas_call(
        functools.partial(front_kernel, chunks, seq),
        in_specs=[anywhere, anywhere, anywhere, inside, anywhere, anywhere, anywhere],
        out_specs=[anywhere, inside, anywhere],
        out_shape=[jax.ShapeDtypeStruct((tok, D), BF16),
                   jax.ShapeDtypeStruct((SUB, tok), F32),
                   jax.ShapeDtypeStruct((seq, 16, width), BF16)],
        scratch_shapes=[pltpu.VMEM((tok, D), BF16), pltpu.VMEM((tok, D), BF16), pltpu.VMEM((D, D), BF16),
                        pltpu.VMEM((3, tok // DIL, SUB, D), BF16), pltpu.VMEM((tok, D), BF16),
                        pltpu.VMEM((seq, 16, width), BF16), pltpu.VMEM((D, D), F32),
                        pltpu.SemaphoreType.DMA((8,)), pltpu.SemaphoreType.DMA((chunks + 3,))],
        compiler_params=pltpu.CompilerParams(vmem_limit_bytes=VMEM),
        cost_estimate=pl.CostEstimate(flops=4 * tok * D * D, bytes_accessed=9 * 10 ** 6, transcendentals=0),
    )(saved, grad, w, lse, view(q), view(k), view(v))


def local_kernel(chunk, first, q_ref, k_ref, v_ref, g_ref, lse_ref, delta_ref, *rest):
    dq_ref, dk_ref, dv_ref, sums_ref = rest[-4:]
    pair = first + pl.program_id(0)
    q2, k2, v2, g2 = q_ref[...], k_ref[...], v_ref[...], g_ref[...]
    tok = q2.shape[0]
    lane = iota((1, 128), 1)
    k_turned = k2.T
    zero = jnp.zeros((), BF16)
    qm = [jnp.where(lane < HW, q2, zero), jnp.where(lane >= HW, q2, zero)]
    gm = [jnp.where(lane < HW, g2, zero), jnp.where(lane >= HW, g2, zero)]
    grad_k = grad_v = None
    grad_q = []
    for c in range(tok // chunk):
        part = slice(c * chunk, (c + 1) * chunk)
        turned = []
        for h in range(2):
            qc, gc = qm[h][part], gm[h][part]
            lse = lse_ref[2 * pair + h, :, part] * LOG2E
            delta = delta_ref[pl.ds(2 * pair + h, 1), part]
            prob = jnp.exp2(dot(k2, qc, 1, 1) * (SCALE * LOG2E) - lse)
            dscore = (prob * (dot(v2, gc, 1, 1) - delta)).astype(BF16)
            weight = prob.astype(BF16)
            a, b = dot(dscore, qc, 1, 0), dot(weight, gc, 1, 0)
            grad_k = a if grad_k is None else grad_k + a
            grad_v = b if grad_v is None else grad_v + b
            turned.append(dot(k_turned[HW * h:HW * h + HW], dscore, 1, 0))
        grad_q.append(jnp.concatenate(turned, axis=0).T)
    grad_q = jnp.concatenate(grad_q, axis=0) * SCALE
    grad_k = grad_k * SCALE
    groups = tok // DIL
    keep = iota((1, DIL, 128), 1) == 2 * pair + iota((1, DIL, 128), 2) // HW
    for i, (out, val) in enumerate(((dq_ref, grad_q), (dk_ref, grad_k), (dv_ref, grad_v))):
        out[...] = val.astype(BF16)
        sums_ref[groups * i:groups * (i + 1)] = jnp.sum(
            jnp.where(keep, val.reshape(groups, DIL, 128), 0.0), axis=1)


def local_level(first, count, q, k, v, g, lse, delta, before=(), after=None):
    tok = q.shape[0]
    col = pl.BlockSpec((tok, 128), lambda i: (0, first + i))
    sums = pl.BlockSpec((3 * (tok // DIL), 128), lambda i: (0, first + i))
    extra = list(before) + ([] if after is None else [after])
    return pl.pallas_call(
        functools.partial(local_kernel, 256, first),
        grid=(count,),
        in_specs=[col] * 4 + [pl.BlockSpec((HEADS, 1, tok), lambda i: (0, 0, 0)),
                              pl.BlockSpec((SUB, tok), lambda i: (0, 0))]
        + [pl.BlockSpec(memory_space=pl.ANY)] * len(extra),
        out_specs=[col] * 3 + [sums],
        out_shape=[jax.ShapeDtypeStruct((tok, D), BF16)] * 3
        + [jax.ShapeDtypeStruct((3 * (tok // DIL), D), F32)],
        input_output_aliases={6 + i: i for i in range(len(before))},
        compiler_params=pltpu.CompilerParams(vmem_limit_bytes=VMEM),
        cost_estimate=pl.CostEstimate(flops=20 * count * tok * tok * HW * 2, bytes_accessed=2 * count * 10 ** 6,
                                      transcendentals=2 * count * tok * tok),
    )(q, k, v, g, lse, delta, *extra)


def dilated_kernel(place, recv_hbm, own_ref, mate_ref, after, sum_ref, mine_ref, theirs_ref,
                   rows_ref, terms_ref, sems):
    loads = [pltpu.make_async_copy(recv_hbm.at[:, :, pl.ds(0, PROJ)], rows_ref, sems.at[0]),
             pltpu.make_async_copy(recv_hbm.at[:, :, pl.ds(PROJ, TERM)], terms_ref, sems.at[1])]
    for load in loads:
        load.start()
    loads[0].wait()
    every = rows_ref[...].astype(F32)
    count = every.shape[0] * 8
    top = every[:, :8].reshape(count, PROJ)
    bot = every[:, 8:].reshape(count, PROJ)
    q, k = top[:, :HALF].astype(BF16), top[:, HALF:STAT].astype(BF16)
    v, g = bot[:, :HALF].astype(BF16), bot[:, HALF:STAT].astype(BF16)
    lse = join_terms(top[:, STAT:]).T[:PART]
    delta = join_terms(bot[:, STAT:]).T[:PART]
    own, mate = own_ref[0].astype(F32), mate_ref[0].astype(F32)
    top = jnp.concatenate([own[:8], mate[:8]], axis=0)
    bot = jnp.concatenate([own[8:], mate[8:]], axis=0)
    own_head = iota((PART, 16, HALF), 0) == iota((PART, 16, HALF), 2) // HW

    def by_head(x):
        return jnp.where(own_head, jnp.broadcast_to(x[None], own_head.shape), 0.0).reshape(PART * 16, HALF).astype(BF16)

    def column(x):
        x = jnp.broadcast_to(join_terms(x)[None], (PART, 16, 128))
        x = jnp.where(iota(x.shape, 0) == iota(x.shape, 2), x, 0.0)
        return jnp.sum(x.reshape(PART * 16, 128), axis=1, keepdims=True)

    def row(x):
        return jnp.broadcast_to(x[:, None], (PART, 16, count)).reshape(PART * 16, count)

    def back(x):
        return jnp.sum(jnp.where(own_head, x.reshape(PART, 16, HALF), 0.0), axis=0)

    def pieces(left_s, right_s, left_p, right_p, lse, delta):
        prob = jnp.exp2(dot(left_s, right_s, 1, 1) * (SCALE * LOG2E) - lse * LOG2E)
        dscore = (prob * (dot(left_p, right_p, 1, 1) - delta)).astype(BF16)
        return prob.astype(BF16), dscore

    _, dscore = pieces(by_head(top[:, :HALF]), k, by_head(bot[:, HALF:STAT]), v,
                       column(top[:, STAT:]), column(bot[:, STAT:]))
    grad_q = back(dot(dscore, k, 1, 0)) * SCALE
    weight, dscore = pieces(by_head(top[:, HALF:STAT]), q, by_head(bot[:, :HALF]), g, row(lse), row(delta))
    grad_k = back(dot(dscore, q, 1, 0)) * SCALE
    grad_v = back(dot(weight, g, 1, 0))
    for i, grad in enumerate((grad_q, grad_k, grad_v)):
        mine_ref[:, HALF * i:HALF * (i + 1)] = grad[:8]
        theirs_ref[:, HALF * i:HALF * (i + 1)] = grad[8:]
    loads[1].wait()
    total = jnp.sum(terms_ref[...].astype(F32), axis=0)
    sum_ref[:16] = total[:, :D]
    sum_ref[16:, :D // 2] = total[:8, D:]
    sum_ref[16:, D // 2:] = total[8:, D:]


def dilated_level(recv, me, after):
    seq = recv.shape[0]
    place = jnp.reshape(me, (1,))
    whole = pl.BlockSpec((8, 3 * HALF), lambda i, p: (0, 0))
    return pl.pallas_call(
        dilated_kernel,
        grid_spec=pltpu.PrefetchScalarGridSpec(
            num_scalar_prefetch=1,
            grid=(1,),
            in_specs=[pl.BlockSpec(memory_space=pl.ANY),
                      pl.BlockSpec((1, 16, PROJ), lambda i, p: (p[0], 0, 0)),
                      pl.BlockSpec((1, 16, PROJ), lambda i, p: (p[0] ^ MATE, 0, 0)),
                      pl.BlockSpec(memory_space=pl.ANY)],
            out_specs=[pl.BlockSpec((24, D), lambda i, p: (0, 0)), whole, whole],
            scratch_shapes=[pltpu.VMEM((seq, 16, PROJ), BF16), pltpu.VMEM((seq, 16, TERM), BF16),
                            pltpu.SemaphoreType.DMA((2,))]),
        out_shape=[jax.ShapeDtypeStruct((24, D), F32)] + [jax.ShapeDtypeStruct((8, 3 * HALF), F32)] * 2,
        compiler_params=pltpu.CompilerParams(vmem_limit_bytes=VMEM),
        cost_estimate=pl.CostEstimate(flops=7 * 2 * 96 * 256 * HALF, bytes_accessed=3 * 10 ** 6,
                                      transcendentals=2 * 96 * 256),
    )(place, recv, recv, recv, after)


def last_kernel(scale, place, mine_ref, theirs_ref, sums_ref, a_ref, b_ref, c_ref, d_ref,
                dq_in, dk_in, dv_in, dq_ref, dk_ref, dv_ref, proj_ref):
    proj_ref[...] = ((a_ref[...] + b_ref[...]) + (c_ref[...] + d_ref[...])) * scale
    first = place[0] & MATE == 0
    here = iota((8, SUB, D), 1) == iota((8, SUB, D), 2) // HW
    for i, (old, out) in enumerate(((dq_in, dq_ref), (dk_in, dk_ref), (dv_in, dv_ref))):
        part = slice(HALF * i, HALF * (i + 1))
        mine, theirs = mine_ref[:, part], theirs_ref[:, part]
        total = sums_ref[8 * i:8 * (i + 1)] + jnp.concatenate([jnp.where(first, mine, theirs), jnp.where(first, theirs, mine)], axis=1)
        out[...] = jnp.where(here, jnp.broadcast_to(total[:, None], (8, SUB, D)),
                             old[...].astype(F32)).astype(BF16)


def last(me, mine, theirs, sums, terms, grads, scale):
    tok = grads[0].shape[0]
    place = jnp.reshape(me, (1,))
    sub = pl.BlockSpec((tok // DIL, SUB, D), lambda i, p: (0, 0, 0))

    def whole(x):
        return pl.BlockSpec(x.shape, lambda i, p: (0, 0))

    view = jax.ShapeDtypeStruct((tok // DIL, DIL, D), BF16)
    small = (mine, theirs, sums, *terms)
    return pl.pallas_call(
        functools.partial(last_kernel, scale),
        grid_spec=pltpu.PrefetchScalarGridSpec(
            num_scalar_prefetch=1,
            grid=(1,),
            in_specs=[whole(x) for x in small] + [sub] * 3,
            out_specs=[sub] * 3 + [whole(terms[0])]),
        out_shape=[view] * 3 + [jax.ShapeDtypeStruct(terms[0].shape, F32)],
        input_output_aliases={1 + len(small) + i: i for i in range(3)},
        compiler_params=pltpu.CompilerParams(vmem_limit_bytes=16 * 2 ** 20),
        cost_estimate=pl.CostEstimate(flops=10 ** 6, bytes_accessed=2 * 10 ** 6, transcendentals=0),
    )(place, *small, *[x.reshape(view.shape) for x in grads])


def on_device(queries, key_rows, value_rows, saved_out, logsumexp, out_grad, proj_weight):
    q, k, v = queries[0], key_rows[0], value_rows[0]
    lse = jnp.transpose(logsumexp, (1, 0, 2))
    tok = q.shape[0]
    seq = lax.axis_size("seq")
    rep = lax.axis_size("rep")
    attn, delta, send = front(saved_out[0], out_grad[0], proj_weight, lse, q, k, v, seq)
    recv = lax.all_to_all(send, "seq", 0, 0)
    me = lax.axis_index("seq")
    part = local_level(0, 5, q, k, v, attn, lse, delta)
    term, mine, theirs = dilated_level(recv, me, part[3])

    def other(x, axis, size, bit):
        return lax.ppermute(x, axis, [(i, i ^ bit) for i in range(size)])

    theirs = other(theirs, "seq", seq, MATE)
    terms = (term, *[other(term, "rep", rep, bit) for bit in (2, 1, 3)])
    part = local_level(5, 1, q, k, v, attn, lse, delta, before=part, after=term)
    *outs, projection_gradient = last(me, mine, theirs, part[3], terms, part[:3], 1.0 / math.sqrt(rep * seq * tok))
    return (*[x.reshape(1, tok, D) for x in outs], projection_gradient)


def solution(mesh):
    rows = P("rep", "seq", None)
    return jax.shard_map(
        on_device,
        mesh=mesh,
        in_specs=(rows, rows, rows, rows, P("rep", None, "seq"), rows, P()),
        out_specs=(rows, rows, rows, P("seq", None)),
        check_vma=False,
    )
```

time: 75.8 us -> 68.1 us (0.90)
  waiting for transfers between devices: 5.04 us -> 0.36 us
  local copies, waits for them, and re-layouts: 2.21 us -> 0.89 us
  Pallas kernels: 51.8 us -> 50.7 us
    all_to_all x1, waiting for transfers between devices: 5.03 us -> 0.35 us  [on_device(): recv = lax.all_to_all(send, 'seq', 0, 0)]
    unnamed x10 -> x6, local copies, waits for them, and re-layouts: 2.21 us -> 0.89 us
  transfers between devices with their start and end apart: 5 -> 5, of which waited for: 1 -> 1; matrix products, arithmetic and copies ran while one was open for 1% -> 0% of each run, Pallas kernels for 48% -> 53%
where the time goes in v4:
time: 68.1 us; the launch traced here: 67.7 us
  Pallas kernels  50.7 us (74%)
  starting transfers between devices  15 us (22%)
  local copies, waits for them, and re-layouts  0.89 us (1%)
  between operations  0.72 us (1%)
    pallas_call x2, Pallas kernels, local_level(): pl.pallas_call(functools.partial(local_kernel, 256, first), grid=(count,)...  36.2 us
    all_to_all x1, starting transfers between devices, on_device(): recv = lax.all_to_all(send, 'seq', 0, 0)  9.54 us
    pallas_call x1, Pallas kernels, front(): pl.pallas_call(functools.partial(front_kernel, chunks, seq), in_specs=[an...  9 us
    ppermute x4, starting transfers between devices, other(): return lax.ppermute(x, axis, [(i, i ^ bit) for i in range(size)])  5.47 us
    pallas_call x1, Pallas kernels, dilated_level(): pl.pallas_call(dilated_kernel, grid_spec=pltpu.PrefetchScalarGridSpec(num...  3.47 us
    pallas_call x1, Pallas kernels, last(): pl.pallas_call(functools.partial(last_kernel, scale), grid_spec=pltpu.Pre...  2.07 us
  transfers between devices with their start and end apart: 5, of which 1 were waited for; matrix products, arithmetic and copies ran while one was open for 0% of the time, Pallas kernels for 53%

profile of v4, /device:TPU:2, one launch (start us, length us, event | category | flops | bytes accessed | tf_op | source)
XLA Modules:
  0.0 67.7 jit_solution(11593634343186911564)
XLA Ops:
  0.6 9.0 %shard_map.102 = (bf16[1024,768]{1,0:T(8,128)(2,1)}, f32[16,1024]{1,0:T(8,128)}, bf16[32,16,2048]{2,1,0:T(8,128)(2,1)}) custom-call(bf16[1024,768]{1,0:T(8,128)(2,1)} %bitcast.31, bf16[1024,768]{1,0:T(8,128)(2,1)} %bitcast.32, bf16[768,768]{1,0:T(8,128)(2,1)} %w_hbm.1, f32[12,1,1024]{2,1,0:T(1,128)} %bitcast.33, bf16[8,128,768]{2,1,0:T(8,128)(2,1)} %bitcast.22, ...), custom_call_target="tpu_custom_call" | custom-call | flops 2415919104 | bytes 9000000 | tf_op jit(solution)/shard_map/pallas_call | solution.py:145
  9.6 9.5 %all-to-all-start = ((bf16[32,16,2048]{2,1,0:T(8,128)(2,1)}), bf16[32,16,2048]{2,1,0:T(8,128)(2,1)}, u32[]{:S(2)}, u32[]{:S(2)}) async-start(bf16[32,16,2048]{2,1,0:T(8,128)(2,1)} %get-tuple-element.22), calls=%async_computation | async-start | bytes 4194304 | tf_op jit(solution)/shard_map/all_to_all | solution.py:341
  19.2 28.8 %shard_map.103 = (bf16[1024,768]{1,0:T(8,128)(2,1)}, bf16[1024,768]{1,0:T(8,128)(2,1)}, bf16[1024,768]{1,0:T(8,128)(2,1)}, f32[24,768]{1,0:T(8,128)}) custom-call(bf16[1024,768]{1,0:T(8,128)(2,1)} %bitcast.23, bf16[1024,768]{1,0:T(8,128)(2,1)} %bitcast.26, bf16[1024,768]{1,0:T(8,128)(2,1)} %bitcast.29, bf16[1024,768]{1,0:T(8,128)(2,1)} %get-tuple-element.23.g_ref, ...), custom_call_target="tpu_custom_call" | custom-call | flops 13421772800 | bytes 10000000 | tf_op jit(solution)/shard_map/pallas_call | solution.py:203
  48.0 0.3 all-to-all-done.recv_hbm.own_ref.mate_ref
  48.4 3.5 %shard_map.104 = (f32[24,768]{1,0:T(8,128)}, f32[8,1152]{1,0:T(8,128)}, f32[8,1152]{1,0:T(8,128)}) custom-call(s32[1]{0:T(128)} %bitcast.place, bf16[32,16,2048]{2,1,0:T(8,128)(2,1)} %all-to-all-done.recv_hbm.own_ref.mate_ref, bf16[32,16,2048]{2,1,0:T(8,128)(2,1)} %all-to-all-done.recv_hbm.own_ref.mate_ref, ...), custom_call_target="tpu_custom_call" | custom-call | flops 132120576 | bytes 3000000 | tf_op jit(solution)/shard_map/pallas_call | solution.py:278
  51.9 1.5 %collective-permute-start.3 = (f32[24,768]{1,0:T(8,128)}, f32[24,768]{1,0:T(8,128)S(1)}, u32[]{:S(2)}, u32[]{:S(2)}) collective-permute-start(f32[24,768]{1,0:T(8,128)} %get-tuple-element.31.rest_4_.a_ref), channel_id=1, source_target_pairs={{0,3},{1,2},{2,1},{3,0},{4,7},{5,6},{6,5},{7,4},{8,11},{9,10},{10,... | collective-permute-start | bytes 221192 | tf_op jit(solution)/shard_map/ppermute | solution.py:347
  53.4 1.6 %collective-permute-start.2 = (f32[24,768]{1,0:T(8,128)}, f32[24,768]{1,0:T(8,128)S(1)}, u32[]{:S(2)}, u32[]{:S(2)}) collective-permute-start(f32[24,768]{1,0:T(8,128)} %get-tuple-element.31.rest_4_.a_ref), channel_id=1, source_target_pairs={{0,1},{1,0},{2,3},{3,2},{4,5},{5,4},{6,7},{7,6},{8,9},{9,8},{10,11... | collective-permute-start | bytes 221192 | tf_op jit(solution)/shard_map/ppermute | solution.py:347
  55.0 0.6 collective-permute-start.1
  55.6 1.7 %collective-permute-start = (f32[8,1152]{1,0:T(8,128)}, f32[8,1152]{1,0:T(8,128)S(1)}, u32[]{:S(2)}, u32[]{:S(2)}) collective-permute-start(f32[8,1152]{1,0:T(8,128)} %get-tuple-element.27), channel_id=1, source_target_pairs={{0,16},{4,20},{8,24},{12,28},{16,0},{20,4},{24,8},{28,12},{32,48},... | collective-permute-start | bytes 110600 | tf_op jit(solution)/shard_map/ppermute | solution.py:347
  57.3 0.0 copy-start.1
  57.3 0.0 copy-start.2
  57.3 7.3 %shard_map.105 = (bf16[1024,768]{1,0:T(8,128)(2,1)}, bf16[1024,768]{1,0:T(8,128)(2,1)}, bf16[1024,768]{1,0:T(8,128)(2,1)}, f32[24,768]{1,0:T(8,128)}) custom-call(bf16[1024,768]{1,0:T(8,128)(2,1)} %bitcast.24, bf16[1024,768]{1,0:T(8,128)(2,1)} %bitcast.27, ...), custom_call_target="tpu_custom_call", output_to_operand_aliasing={{0}: (6, {}), {1}: (7, {}), {2}: (8, {}), {3}: (9, {})} | custom-call | flops 2684354560 | bytes 2000000 | tf_op jit(solution)/shard_map/pallas_call | solution.py:203
  64.7 0.0 collective-permute-done.theirs_ref
  64.7 0.0 collective-permute-done.3.d_ref
  64.7 0.0 collective-permute-done.2.c_ref
  64.7 0.0 collective-permute-done.1.b_ref
  64.7 0.0 copy-done.1
  64.7 0.0 copy-done.2
  64.7 0.0 copy-start
  64.7 0.9 %copy-done = f32[24,768]{1,0:T(8,128)S(1)} copy-done((f32[24,768]{1,0:T(8,128)S(1)}, f32[24,768]{1,0:T(8,128)}, u32[]{:S(2)}) %copy-start) | copy-done | bytes 73752
  65.6 2.1 %shard_map.106 = (bf16[8,128,768]{2,1,0:T(8,128)(2,1)}, bf16[8,128,768]{2,1,0:T(8,128)(2,1)}, bf16[8,128,768]{2,1,0:T(8,128)(2,1)}, f32[24,768]{1,0:T(8,128)}) custom-call(s32[1]{0:T(128)} %bitcast.place, f32[8,1152]{1,0:T(8,128)S(1)} %copy-done.2, ...), custom_call_target="tpu_custom_call", output_to_operand_aliasing={{0}: (8, {}), {1}: (9, {}), {2}: (10, {})} | custom-call | flops 1000000 | bytes 2000000 | tf_op jit(solution)/shard_map/pallas_call | solution.py:320
Async XLA Ops:
  9.6 38.7 %all-to-all-start = ((bf16[32,16,2048]{2,1,0:T(8,128)(2,1)}), bf16[32,16,2048]{2,1,0:T(8,128)(2,1)}, u32[]{:S(2)}, u32[]{:S(2)}) async-start(bf16[32,16,2048]{2,1,0:T(8,128)(2,1)} %get-tuple-element.22), calls=%async_computation | async-start | bytes 4194304 | tf_op jit(solution)/shard_map/all_to_all | solution.py:341
  51.9 12.8 %collective-permute-start.3 = (f32[24,768]{1,0:T(8,128)}, f32[24,768]{1,0:T(8,128)S(1)}, u32[]{:S(2)}, u32[]{:S(2)}) collective-permute-start(f32[24,768]{1,0:T(8,128)} %get-tuple-element.31.rest_4_.a_ref), channel_id=1, source_target_pairs={{0,3},{1,2},{2,1},{3,0},{4,7},{5,6},{6,5},{7,4},{8,11},{9,10},{10,... | collective-permute-start | bytes 221192 | tf_op jit(solution)/shard_map/ppermute | solution.py:347
  53.4 11.3 %collective-permute-start.2 = (f32[24,768]{1,0:T(8,128)}, f32[24,768]{1,0:T(8,128)S(1)}, u32[]{:S(2)}, u32[]{:S(2)}) collective-permute-start(f32[24,768]{1,0:T(8,128)} %get-tuple-element.31.rest_4_.a_ref), channel_id=1, source_target_pairs={{0,1},{1,0},{2,3},{3,2},{4,5},{5,4},{6,7},{7,6},{8,9},{9,8},{10,11... | collective-permute-start | bytes 221192 | tf_op jit(solution)/shard_map/ppermute | solution.py:347
  55.0 9.7 %collective-permute-start.1 = (f32[24,768]{1,0:T(8,128)}, f32[24,768]{1,0:T(8,128)S(1)}, u32[]{:S(2)}, u32[]{:S(2)}) collective-permute-start(f32[24,768]{1,0:T(8,128)} %get-tuple-element.31.rest_4_.a_ref), channel_id=1, source_target_pairs={{0,2},{1,3},{2,0},{3,1},{4,6},{5,7},{6,4},{7,5},{8,10},{9,11},{10,... | collective-permute-start | bytes 221192 | tf_op jit(solution)/shard_map/ppermute | solution.py:347
  55.6 9.1 %collective-permute-start = (f32[8,1152]{1,0:T(8,128)}, f32[8,1152]{1,0:T(8,128)S(1)}, u32[]{:S(2)}, u32[]{:S(2)}) collective-permute-start(f32[8,1152]{1,0:T(8,128)} %get-tuple-element.27), channel_id=1, source_target_pairs={{0,16},{4,20},{8,24},{12,28},{16,0},{20,4},{24,8},{28,12},{32,48},... | collective-permute-start | bytes 110600 | tf_op jit(solution)/shard_map/ppermute | solution.py:347
  57.3 7.4 %copy-start.1 = (f32[24,768]{1,0:T(8,128)S(1)}, f32[24,768]{1,0:T(8,128)}, u32[]{:S(2)}) copy-start(f32[24,768]{1,0:T(8,128)} %get-tuple-element.31.rest_4_.a_ref) | copy-start | bytes 221188
  57.3 7.4 %copy-start.2 = (f32[8,1152]{1,0:T(8,128)S(1)}, f32[8,1152]{1,0:T(8,128)}, u32[]{:S(2)}) copy-start(f32[8,1152]{1,0:T(8,128)} %get-tuple-element.26.mine_ref) | copy-start | bytes 110596
  64.7 0.9 %copy-start = (f32[24,768]{1,0:T(8,128)S(1)}, f32[24,768]{1,0:T(8,128)}, u32[]{:S(2)}) copy-start(f32[24,768]{1,0:T(8,128)} %get-tuple-element.32.sums_ref) | copy-start | bytes 221188

commit v5 on v4

--- a/solution.py
+++ b/solution.py
@@ -51,12 +51,12 @@
     return (x + pltpu.roll(x, 112, 1)) + pltpu.roll(x, 96, 1)
 
 
-def front_kernel(chunks, seq, saved_hbm, grad_hbm, w_hbm, lse_ref, q_hbm, k_hbm, v_hbm,
-                 attn_hbm, delta_ref, send_hbm,
-                 saved_ref, grad_ref, w_ref, pick_ref, attn_ref, send_ref, acc, in_sems, out_sems):
+def front_kernel(seq, saved_hbm, grad_hbm, w_hbm, lse_hbm, q_hbm, k_hbm, v_hbm,
+                 attn_hbm, delta_hbm, send_hbm,
+                 saved_ref, grad_ref, w_ref, lse_ref, pick_ref, attn_ref, delta_ref, send_ref, acc,
+                 in_sems, out_sems):
     tok = saved_ref.shape[0]
-    rows = tok // chunks
-    groups = rows // DIL
+    groups = tok // DIL
     halves = [pl.ds(i * (tok // 2), tok // 2) for i in range(2)]
 
     loads = []
@@ -71,6 +71,7 @@
     load(w_hbm, w_ref)
     for i, x in enumerate((q_hbm, k_hbm, v_hbm)):
         load(x.at[:, pl.ds(0, SUB)], pick_ref.at[i])
+    load(lse_hbm, lse_ref)
 
     stores = []
 
@@ -98,20 +99,18 @@
     loads[4].wait()
     pick = (iota((D, 128), 0) // HW == iota((D, 128), 1)).astype(BF16)
     diag = iota((1, DIL, 128), 1) == iota((1, DIL, 128), 2)
-    picked_g, picked_d = [], []
-    for c in range(chunks):
-        part = pl.ds(c * rows, rows)
-        attn = dot(grad_ref[part], w_ref[...], 1, 1).astype(BF16)
-        attn_ref[part] = attn
-        store(attn_ref.at[part], attn_hbm.at[part])
-        attn = attn.astype(F32)
-        prod = attn * saved_ref[part].astype(F32)
-        hi = prod.astype(BF16)
-        low = (prod - hi.astype(F32)).astype(BF16)
-        delta = dot(hi, pick, 1, 0) + dot(low, pick, 1, 0)
-        delta_ref[:, part] = delta.T[:SUB]
-        picked_g.append(head_rows(attn.reshape(groups, DIL, D)[:, :SUB]))
-        picked_d.append(jnp.sum(jnp.where(diag, delta.reshape(groups, DIL, 128), 0.0), axis=1))
+    attn = dot(grad_ref[...], w_ref[...], 1, 1).astype(BF16)
+    attn_ref[...] = attn
+    store(attn_ref, attn_hbm)
+    attn = attn.astype(F32)
+    prod = attn * saved_ref[...].astype(F32)
+    hi = prod.astype(BF16)
+    low = (prod - hi.astype(F32)).astype(BF16)
+    delta = dot(hi, pick, 1, 0) + dot(low, pick, 1, 0)
+    delta_ref[...] = delta.T[:SUB]
+    store(delta_ref, delta_hbm)
+    picked_g = head_rows(attn.reshape(groups, DIL, D)[:, :SUB])
+    delta = jnp.sum(jnp.where(diag, delta.reshape(groups, DIL, 128), 0.0), axis=1)
 
     for copy in loads[5:]:
         copy.wait()
@@ -119,9 +118,7 @@
     lse = jnp.concatenate(
         [sum(jnp.where(lane == h, lse_ref[h, :, DIL * j:DIL * (j + 1)], 0.0) for h in range(HEADS))
          for j in range(tok // DIL)], axis=0)
-    delta = jnp.concatenate(picked_d, axis=0)
-    picked = [head_rows(pick_ref[0]), head_rows(pick_ref[1]), head_rows(pick_ref[2]),
-              jnp.concatenate(picked_g, axis=0)]
+    picked = [head_rows(pick_ref[0]), head_rows(pick_ref[1]), head_rows(pick_ref[2]), picked_g]
     own = []
     for half in range(2):
         q, k, v, g = (x[:, HALF * half:HALF * (half + 1)] for x in picked)
@@ -137,22 +134,21 @@
 
 def front(saved, grad, w, lse, q, k, v, seq):
     tok = saved.shape[0]
-    chunks = 2
     view = lambda x: x.reshape(tok // DIL, DIL, D)
     anywhere = pl.BlockSpec(memory_space=pl.ANY)
-    inside = pl.BlockSpec(memory_space=pltpu.VMEM)
     width = PROJ + TERM
     return pl.pallas_call(
-        functools.partial(front_kernel, chunks, seq),
-        in_specs=[anywhere, anywhere, anywhere, inside, anywhere, anywhere, anywhere],
-        out_specs=[anywhere, inside, anywhere],
+        functools.partial(front_kernel, seq),
+        in_specs=[anywhere] * 7,
+        out_specs=[anywhere] * 3,
         out_shape=[jax.ShapeDtypeStruct((tok, D), BF16),
                    jax.ShapeDtypeStruct((SUB, tok), F32),
                    jax.ShapeDtypeStruct((seq, 16, width), BF16)],
         scratch_shapes=[pltpu.VMEM((tok, D), BF16), pltpu.VMEM((tok, D), BF16), pltpu.VMEM((D, D), BF16),
-                        pltpu.VMEM((3, tok // DIL, SUB, D), BF16), pltpu.VMEM((tok, D), BF16),
+                        pltpu.VMEM((HEADS, 1, tok), F32), pltpu.VMEM((3, tok // DIL, SUB, D), BF16),
+                        pltpu.VMEM((tok, D), BF16), pltpu.VMEM((SUB, tok), F32),
                         pltpu.VMEM((seq, 16, width), BF16), pltpu.VMEM((D, D), F32),
-                        pltpu.SemaphoreType.DMA((8,)), pltpu.SemaphoreType.DMA((chunks + 3,))],
+                        pltpu.SemaphoreType.DMA((9,)), pltpu.SemaphoreType.DMA((5,))],
         compiler_params=pltpu.CompilerParams(vmem_limit_bytes=VMEM),
         cost_estimate=pl.CostEstimate(flops=4 * tok * D * D, bytes_accessed=9 * 10 ** 6, transcendentals=0),
     )(saved, grad, w, lse, view(q), view(k), view(v))
@@ -165,28 +161,38 @@
     tok = q2.shape[0]
     lane = iota((1, 128), 1)
     k_turned = k2.T
-    zero = jnp.zeros((), BF16)
-    qm = [jnp.where(lane < HW, q2, zero), jnp.where(lane >= HW, q2, zero)]
-    gm = [jnp.where(lane < HW, g2, zero), jnp.where(lane >= HW, g2, zero)]
+
+    def stacked(x):
+        zero = jnp.zeros((), BF16)
+        return jnp.concatenate([jnp.where(lane < HW, x, zero), jnp.where(lane >= HW, x, zero)], axis=0)
+
+    def chosen(x):
+        return jnp.where(lane < HW, x[:tok], x[tok:])
+
+    k_stack, v_stack = stacked(k2), stacked(v2)
     grad_k = grad_v = None
     grad_q = []
     for c in range(tok // chunk):
         part = slice(c * chunk, (c + 1) * chunk)
-        turned = []
+        scores = dot(k_stack, q2[part], 1, 1)
+        dprobs = dot(v_stack, g2[part], 1, 1)
+        dscores, weights, turned = [], [], []
         for h in range(2):
-            qc, gc = qm[h][part], gm[h][part]
+            rows = slice(tok * h, tok * (h + 1))
             lse = lse_ref[2 * pair + h, :, part] * LOG2E
             delta = delta_ref[pl.ds(2 * pair + h, 1), part]
-            prob = jnp.exp2(dot(k2, qc, 1, 1) * (SCALE * LOG2E) - lse)
-            dscore = (prob * (dot(v2, gc, 1, 1) - delta)).astype(BF16)
-            weight = prob.astype(BF16)
-            a, b = dot(dscore, qc, 1, 0), dot(weight, gc, 1, 0)
-            grad_k = a if grad_k is None else grad_k + a
-            grad_v = b if grad_v is None else grad_v + b
-            turned.append(dot(k_turned[HW * h:HW * h + HW], dscore, 1, 0))
+            prob = jnp.exp2(scores[rows] * (SCALE * LOG2E) - lse)
+            dscores.append((prob * (dprobs[rows] - delta)).astype(BF16))
+            weights.append(prob.astype(BF16))
+            turned.append(dot(k_turned[HW * h:HW * h + HW], dscores[h], 1, 0))
+        a = dot(jnp.concatenate(dscores, axis=0), q2[part], 1, 0)
+        b = dot(jnp.concatenate(weights, axis=0), g2[part], 1, 0)
+        grad_k = a if grad_k is None else grad_k + a
+        grad_v = b if grad_v is None else grad_v + b
         grad_q.append(jnp.concatenate(turned, axis=0).T)
     grad_q = jnp.concatenate(grad_q, axis=0) * SCALE
-    grad_k = grad_k * SCALE
+    grad_k = chosen(grad_k) * SCALE
+    grad_v = chosen(grad_v)
     groups = tok // DIL
     keep = iota((1, DIL, 128), 1) == 2 * pair + iota((1, DIL, 128), 2) // HW
     for i, (out, val) in enumerate(((dq_ref, grad_q), (dk_ref, grad_k), (dv_ref, grad_v))):
@@ -216,7 +222,7 @@
     )(q, k, v, g, lse, delta, *extra)
 
 
-def dilated_kernel(place, recv_hbm, own_ref, mate_ref, after, sum_ref, mine_ref, theirs_ref,
+def dilated_kernel(place, recv_hbm, after, sum_ref, mine_ref, theirs_ref,
                    rows_ref, terms_ref, sems):
     loads = [pltpu.make_async_copy(recv_hbm.at[:, :, pl.ds(0, PROJ)], rows_ref, sems.at[0]),
              pltpu.make_async_copy(recv_hbm.at[:, :, pl.ds(PROJ, TERM)], terms_ref, sems.at[1])]
@@ -231,7 +237,7 @@
     v, g = bot[:, :HALF].astype(BF16), bot[:, HALF:STAT].astype(BF16)
     lse = join_terms(top[:, STAT:]).T[:PART]
     delta = join_terms(bot[:, STAT:]).T[:PART]
-    own, mate = own_ref[0].astype(F32), mate_ref[0].astype(F32)
+    own, mate = rows_ref[place[0]].astype(F32), rows_ref[place[0] ^ MATE].astype(F32)
     top = jnp.concatenate([own[:8], mate[:8]], axis=0)
     bot = jnp.concatenate([own[8:], mate[8:]], axis=0)
     own_head = iota((PART, 16, HALF), 0) == iota((PART, 16, HALF), 2) // HW
@@ -280,10 +286,7 @@
         grid_spec=pltpu.PrefetchScalarGridSpec(
             num_scalar_prefetch=1,
             grid=(1,),
-            in_specs=[pl.BlockSpec(memory_space=pl.ANY),
-                      pl.BlockSpec((1, 16, PROJ), lambda i, p: (p[0], 0, 0)),
-                      pl.BlockSpec((1, 16, PROJ), lambda i, p: (p[0] ^ MATE, 0, 0)),
-                      pl.BlockSpec(memory_space=pl.ANY)],
+            in_specs=[pl.BlockSpec(memory_space=pl.ANY)] * 2,
             out_specs=[pl.BlockSpec((24, D), lambda i, p: (0, 0)), whole, whole],
             scratch_shapes=[pltpu.VMEM((seq, 16, PROJ), BF16), pltpu.VMEM((seq, 16, TERM), BF16),
                             pltpu.SemaphoreType.DMA((2,))]),
@@ -291,14 +294,17 @@
         compiler_params=pltpu.CompilerParams(vmem_limit_bytes=VMEM),
         cost_estimate=pl.CostEstimate(flops=7 * 2 * 96 * 256 * HALF, bytes_accessed=3 * 10 ** 6,
                                       transcendentals=2 * 96 * 256),
-    )(place, recv, recv, recv, after)
-
-
-def last_kernel(scale, place, mine_ref, theirs_ref, sums_ref, a_ref, b_ref, c_ref, d_ref,
-                dq_in, dk_in, dv_in, dq_ref, dk_ref, dv_ref, proj_ref):
+    )(place, recv, after)
+
+
+def last_kernel(scale, place, mine_ref, theirs_ref, a_ref, b_ref, c_ref, d_ref, sums_hbm,
+                dq_in, dk_in, dv_in, dq_ref, dk_ref, dv_ref, proj_ref, sums_ref, sem):
+    load = pltpu.make_async_copy(sums_hbm, sums_ref, sem)
+    load.start()
     proj_ref[...] = ((a_ref[...] + b_ref[...]) + (c_ref[...] + d_ref[...])) * scale
     first = place[0] & MATE == 0
     here = iota((8, SUB, D), 1) == iota((8, SUB, D), 2) // HW
+    load.wait()
     for i, (old, out) in enumerate(((dq_in, dq_ref), (dk_in, dk_ref), (dv_in, dv_ref))):
         part = slice(HALF * i, HALF * (i + 1))
         mine, theirs = mine_ref[:, part], theirs_ref[:, part]
@@ -316,19 +322,20 @@
         return pl.BlockSpec(x.shape, lambda i, p: (0, 0))
 
     view = jax.ShapeDtypeStruct((tok // DIL, DIL, D), BF16)
-    small = (mine, theirs, sums, *terms)
+    small = (mine, theirs, *terms)
     return pl.pallas_call(
         functools.partial(last_kernel, scale),
         grid_spec=pltpu.PrefetchScalarGridSpec(
             num_scalar_prefetch=1,
             grid=(1,),
-            in_specs=[whole(x) for x in small] + [sub] * 3,
-            out_specs=[sub] * 3 + [whole(terms[0])]),
+            in_specs=[whole(x) for x in small] + [pl.BlockSpec(memory_space=pl.ANY)] + [sub] * 3,
+            out_specs=[sub] * 3 + [whole(terms[0])],
+            scratch_shapes=[pltpu.VMEM(sums.shape, F32), pltpu.SemaphoreType.DMA(())]),
         out_shape=[view] * 3 + [jax.ShapeDtypeStruct(terms[0].shape, F32)],
-        input_output_aliases={1 + len(small) + i: i for i in range(3)},
+        input_output_aliases={2 + len(small) + i: i for i in range(3)},
         compiler_params=pltpu.CompilerParams(vmem_limit_bytes=16 * 2 ** 20),
         cost_estimate=pl.CostEstimate(flops=10 ** 6, bytes_accessed=2 * 10 ** 6, transcendentals=0),
-    )(place, *small, *[x.reshape(view.shape) for x in grads])
+    )(place, *small, sums, *[x.reshape(view.shape) for x in grads])
 
 
 def on_device(queries, key_rows, value_rows, saved_out, logsumexp, out_grad, proj_weight):

time: 68.1 us -> 66.9 us (0.982)
  Pallas kernels: 50.7 us -> 49.2 us
    pallas_call x1, Pallas kernels: 3.47 us -> 2.7 us  [dilated_level(): pl.pallas_call(dilated_kernel, grid_spec=pltpu.PrefetchScalarGridSpec(num...]
  transfers between devices with their start and end apart: 5 -> 5, of which waited for: 1 -> 1; matrix products, arithmetic and copies ran while one was open for 0% -> 0% of each run, Pallas kernels for 53% -> 54%
where the time goes in v5:
time: 66.9 us; the launch traced here: 66.6 us
  Pallas kernels  49.2 us (74%)
  starting transfers between devices  15 us (22%)
  local copies, waits for them, and re-layouts  0.89 us (1%)
  between operations  0.87 us (1%)
    pallas_call x2, Pallas kernels, local_level(): pl.pallas_call(functools.partial(local_kernel, 256, first), grid=(count,)...  35.8 us
    all_to_all x1, starting transfers between devices, on_device(): recv = lax.all_to_all(send, 'seq', 0, 0)  9.56 us
    pallas_call x1, Pallas kernels, front(): pl.pallas_call(functools.partial(front_kernel, seq), in_specs=[anywhere]...  8.51 us
    ppermute x4, starting transfers between devices, other(): return lax.ppermute(x, axis, [(i, i ^ bit) for i in range(size)])  5.43 us
    pallas_call x1, Pallas kernels, dilated_level(): pl.pallas_call(dilated_kernel, grid_spec=pltpu.PrefetchScalarGridSpec(num...  2.7 us
    pallas_call x1, Pallas kernels, last(): pl.pallas_call(functools.partial(last_kernel, scale), grid_spec=pltpu.Pre...  2.14 us
  transfers between devices with their start and end apart: 5, of which 1 were waited for; matrix products, arithmetic and copies ran while one was open for 0% of the time, Pallas kernels for 54%

profile of v5, /device:TPU:2, one launch (start us, length us, event | category | flops | bytes accessed | tf_op | source)
XLA Modules:
  0.0 66.6 jit_solution(957216193845993196)
XLA Ops:
  0.6 8.5 %shard_map.102 = (bf16[1024,768]{1,0:T(8,128)(2,1)}, f32[16,1024]{1,0:T(8,128)}, bf16[32,16,2048]{2,1,0:T(8,128)(2,1)}) custom-call(bf16[1024,768]{1,0:T(8,128)(2,1)} %bitcast.31, bf16[1024,768]{1,0:T(8,128)(2,1)} %bitcast.32, bf16[768,768]{1,0:T(8,128)(2,1)} %w_hbm.1, f32[12,1,1024]{2,1,0:T(1,128)} %bitcast.33, bf16[8,128,768]{2,1,0:T(8,128)(2,1)} %bitcast.22, ...), custom_call_target="tpu_custom_call" | custom-call | flops 2415919104 | bytes 9000000 | tf_op jit(solution)/shard_map/pallas_call | solution.py:140
  9.1 9.6 %all-to-all-start = ((bf16[32,16,2048]{2,1,0:T(8,128)(2,1)}), bf16[32,16,2048]{2,1,0:T(8,128)(2,1)}, u32[]{:S(2)}, u32[]{:S(2)}) async-start(bf16[32,16,2048]{2,1,0:T(8,128)(2,1)} %get-tuple-element.22), calls=%async_computation | async-start | bytes 4194304 | tf_op jit(solution)/shard_map/all_to_all | solution.py:348
  18.7 28.5 %shard_map.103 = (bf16[1024,768]{1,0:T(8,128)(2,1)}, bf16[1024,768]{1,0:T(8,128)(2,1)}, bf16[1024,768]{1,0:T(8,128)(2,1)}, f32[24,768]{1,0:T(8,128)}) custom-call(bf16[1024,768]{1,0:T(8,128)(2,1)} %bitcast.23, bf16[1024,768]{1,0:T(8,128)(2,1)} %bitcast.26, bf16[1024,768]{1,0:T(8,128)(2,1)} %bitcast.29, bf16[1024,768]{1,0:T(8,128)(2,1)} %get-tuple-element.23.g_ref, ...), custom_call_target="tpu_custom_call" | custom-call | flops 13421772800 | bytes 10000000 | tf_op jit(solution)/shard_map/pallas_call | solution.py:209
  47.2 0.6 all-to-all-done.recv_hbm
  47.9 2.7 %shard_map.104 = (f32[24,768]{1,0:T(8,128)}, f32[8,1152]{1,0:T(8,128)}, f32[8,1152]{1,0:T(8,128)}) custom-call(s32[1]{0:T(128)} %bitcast.place, bf16[32,16,2048]{2,1,0:T(8,128)(2,1)} %all-to-all-done.recv_hbm, f32[24,768]{1,0:T(8,128)} %get-tuple-element.25.after.rest_3_), custom_call_target="tpu_custom_call" | custom-call | flops 132120576 | bytes 3000000 | tf_op jit(solution)/shard_map/pallas_call | solution.py:284
  50.6 1.2 %collective-permute-start.3 = (f32[24,768]{1,0:T(8,128)}, f32[24,768]{1,0:T(8,128)S(1)}, u32[]{:S(2)}, u32[]{:S(2)}) collective-permute-start(f32[24,768]{1,0:T(8,128)} %get-tuple-element.28.rest_4_.a_ref), channel_id=1, source_target_pairs={{0,3},{1,2},{2,1},{3,0},{4,7},{5,6},{6,5},{7,4},{8,11},{9,10},{10,... | collective-permute-start | bytes 221192 | tf_op jit(solution)/shard_map/ppermute | solution.py:354
  51.8 1.9 %collective-permute-start.2 = (f32[24,768]{1,0:T(8,128)}, f32[24,768]{1,0:T(8,128)S(1)}, u32[]{:S(2)}, u32[]{:S(2)}) collective-permute-start(f32[24,768]{1,0:T(8,128)} %get-tuple-element.28.rest_4_.a_ref), channel_id=1, source_target_pairs={{0,1},{1,0},{2,3},{3,2},{4,5},{5,4},{6,7},{7,6},{8,9},{9,8},{10,11... | collective-permute-start | bytes 221192 | tf_op jit(solution)/shard_map/ppermute | solution.py:354
  53.7 0.6 collective-permute-start.1
  54.3 1.7 %collective-permute-start = (f32[8,1152]{1,0:T(8,128)}, f32[8,1152]{1,0:T(8,128)S(1)}, u32[]{:S(2)}, u32[]{:S(2)}) collective-permute-start(f32[8,1152]{1,0:T(8,128)} %get-tuple-element.27), channel_id=1, source_target_pairs={{0,16},{4,20},{8,24},{12,28},{16,0},{20,4},{24,8},{28,12},{32,48},... | collective-permute-start | bytes 110600 | tf_op jit(solution)/shard_map/ppermute | solution.py:354
  56.0 0.0 copy-start.1
  56.0 0.0 copy-start.2
  56.0 7.3 %shard_map.105 = (bf16[1024,768]{1,0:T(8,128)(2,1)}, bf16[1024,768]{1,0:T(8,128)(2,1)}, bf16[1024,768]{1,0:T(8,128)(2,1)}, f32[24,768]{1,0:T(8,128)}) custom-call(bf16[1024,768]{1,0:T(8,128)(2,1)} %bitcast.24, bf16[1024,768]{1,0:T(8,128)(2,1)} %bitcast.27, ...), custom_call_target="tpu_custom_call", output_to_operand_aliasing={{0}: (6, {}), {1}: (7, {}), {2}: (8, {}), {3}: (9, {})} | custom-call | flops 2684354560 | bytes 2000000 | tf_op jit(solution)/shard_map/pallas_call | solution.py:209
  63.3 0.0 collective-permute-done.theirs_ref
  63.3 0.0 collective-permute-done.3.d_ref
  63.4 0.0 collective-permute-done.2.c_ref
  63.4 0.0 collective-permute-done.1.b_ref
  63.4 0.0 copy-done.1
  63.4 0.0 copy-done.2
  63.4 0.0 copy-start
  63.4 0.9 %copy-done = f32[24,768]{1,0:T(8,128)S(1)} copy-done((f32[24,768]{1,0:T(8,128)S(1)}, f32[24,768]{1,0:T(8,128)}, u32[]{:S(2)}) %copy-start) | copy-done | bytes 73752
  64.3 2.1 %shard_map.106 = (bf16[8,128,768]{2,1,0:T(8,128)(2,1)}, bf16[8,128,768]{2,1,0:T(8,128)(2,1)}, bf16[8,128,768]{2,1,0:T(8,128)(2,1)}, f32[24,768]{1,0:T(8,128)}) custom-call(s32[1]{0:T(128)} %bitcast.place, f32[8,1152]{1,0:T(8,128)S(1)} %copy-done.2, ...), custom_call_target="tpu_custom_call", output_to_operand_aliasing={{0}: (8, {}), {1}: (9, {}), {2}: (10, {})} | custom-call | flops 1000000 | bytes 2000000 | tf_op jit(solution)/shard_map/pallas_call | solution.py:326
Async XLA Ops:
  9.1 38.7 %all-to-all-start = ((bf16[32,16,2048]{2,1,0:T(8,128)(2,1)}), bf16[32,16,2048]{2,1,0:T(8,128)(2,1)}, u32[]{:S(2)}, u32[]{:S(2)}) async-start(bf16[32,16,2048]{2,1,0:T(8,128)(2,1)} %get-tuple-element.22), calls=%async_computation | async-start | bytes 4194304 | tf_op jit(solution)/shard_map/all_to_all | solution.py:348
  50.6 12.8 %collective-permute-start.3 = (f32[24,768]{1,0:T(8,128)}, f32[24,768]{1,0:T(8,128)S(1)}, u32[]{:S(2)}, u32[]{:S(2)}) collective-permute-start(f32[24,768]{1,0:T(8,128)} %get-tuple-element.28.rest_4_.a_ref), channel_id=1, source_target_pairs={{0,3},{1,2},{2,1},{3,0},{4,7},{5,6},{6,5},{7,4},{8,11},{9,10},{10,... | collective-permute-start | bytes 221192 | tf_op jit(solution)/shard_map/ppermute | solution.py:354
  51.8 11.5 %collective-permute-start.2 = (f32[24,768]{1,0:T(8,128)}, f32[24,768]{1,0:T(8,128)S(1)}, u32[]{:S(2)}, u32[]{:S(2)}) collective-permute-start(f32[24,768]{1,0:T(8,128)} %get-tuple-element.28.rest_4_.a_ref), channel_id=1, source_target_pairs={{0,1},{1,0},{2,3},{3,2},{4,5},{5,4},{6,7},{7,6},{8,9},{9,8},{10,11... | collective-permute-start | bytes 221192 | tf_op jit(solution)/shard_map/ppermute | solution.py:354
  53.7 9.7 %collective-permute-start.1 = (f32[24,768]{1,0:T(8,128)}, f32[24,768]{1,0:T(8,128)S(1)}, u32[]{:S(2)}, u32[]{:S(2)}) collective-permute-start(f32[24,768]{1,0:T(8,128)} %get-tuple-element.28.rest_4_.a_ref), channel_id=1, source_target_pairs={{0,2},{1,3},{2,0},{3,1},{4,6},{5,7},{6,4},{7,5},{8,10},{9,11},{10,... | collective-permute-start | bytes 221192 | tf_op jit(solution)/shard_map/ppermute | solution.py:354
  54.3 9.0 %collective-permute-start = (f32[8,1152]{1,0:T(8,128)}, f32[8,1152]{1,0:T(8,128)S(1)}, u32[]{:S(2)}, u32[]{:S(2)}) collective-permute-start(f32[8,1152]{1,0:T(8,128)} %get-tuple-element.27), channel_id=1, source_target_pairs={{0,16},{4,20},{8,24},{12,28},{16,0},{20,4},{24,8},{28,12},{32,48},... | collective-permute-start | bytes 110600 | tf_op jit(solution)/shard_map/ppermute | solution.py:354
  56.0 7.4 %copy-start.1 = (f32[24,768]{1,0:T(8,128)S(1)}, f32[24,768]{1,0:T(8,128)}, u32[]{:S(2)}) copy-start(f32[24,768]{1,0:T(8,128)} %get-tuple-element.28.rest_4_.a_ref) | copy-start | bytes 221188
  56.0 7.4 %copy-start.2 = (f32[8,1152]{1,0:T(8,128)S(1)}, f32[8,1152]{1,0:T(8,128)}, u32[]{:S(2)}) copy-start(f32[8,1152]{1,0:T(8,128)} %get-tuple-element.26.mine_ref) | copy-start | bytes 110596
  63.4 0.9 %copy-start = (f32[24,768]{1,0:T(8,128)S(1)}, f32[24,768]{1,0:T(8,128)}, u32[]{:S(2)}) copy-start(f32[24,768]{1,0:T(8,128)} %get-tuple-element.32.sums_hbm) | copy-start | bytes 221188

commit v6 on v5

--- a/solution.py
+++ b/solution.py
@@ -24,6 +24,7 @@
 TERM = D + D // 2
 MATE = 4
 VMEM = 62 * 2 ** 20
+ROOM = 4096
 
 
 def dot(a, b, ca, cb):
@@ -53,11 +54,10 @@
 
 def front_kernel(seq, saved_hbm, grad_hbm, w_hbm, lse_hbm, q_hbm, k_hbm, v_hbm,
                  attn_hbm, delta_hbm, send_hbm,
-                 saved_ref, grad_ref, w_ref, lse_ref, pick_ref, attn_ref, delta_ref, send_ref, acc,
+                 saved_ref, grad_ref, w_ref, lse_ref, pick_ref, attn_ref, delta_ref, send_ref,
                  in_sems, out_sems):
     tok = saved_ref.shape[0]
     groups = tok // DIL
-    halves = [pl.ds(i * (tok // 2), tok // 2) for i in range(2)]
 
     loads = []
 
@@ -65,9 +65,8 @@
         loads.append(pltpu.make_async_copy(source, target, in_sems.at[len(loads)]))
         loads[-1].start()
 
-    for half in halves:
-        load(grad_hbm.at[half], grad_ref.at[half])
-        load(saved_hbm.at[half], saved_ref.at[half])
+    load(grad_hbm, grad_ref)
+    load(saved_hbm, saved_ref)
     load(w_hbm, w_ref)
     for i, x in enumerate((q_hbm, k_hbm, v_hbm)):
         load(x.at[:, pl.ds(0, SUB)], pick_ref.at[i])
@@ -79,41 +78,23 @@
         stores.append(pltpu.make_async_copy(source, target, out_sems.at[len(stores)]))
         stores[-1].start()
 
-    loads[0].wait()
-    loads[1].wait()
-    acc[...] = dot(saved_ref[halves[0]], grad_ref[halves[0]], 0, 0)
-    loads[2].wait()
-    loads[3].wait()
-    share = D // seq
-    for i in range(2):
-        wide = slice(HALF * i, HALF * (i + 1))
-        term = acc[wide] + dot(saved_ref[halves[1], wide], grad_ref[halves[1]], 0, 0)
-        for s in range(seq // 2):
-            here = send_ref.at[i * (seq // 2) + s]
-            here[:, PROJ:PROJ + D] = term[share * s:share * s + 16].astype(BF16)
-            rest = term[share * s + 16:share * s + 24]
-            here[:, PROJ + D:] = jnp.concatenate([rest[:, :D // 2], rest[:, D // 2:]], axis=0).astype(BF16)
-        some = (pl.ds(i * (seq // 2), seq // 2), slice(None), pl.ds(PROJ, TERM))
-        store(send_ref.at[some], send_hbm.at[some])
-
-    loads[4].wait()
+    for copy in loads:
+        copy.wait()
     pick = (iota((D, 128), 0) // HW == iota((D, 128), 1)).astype(BF16)
     diag = iota((1, DIL, 128), 1) == iota((1, DIL, 128), 2)
     attn = dot(grad_ref[...], w_ref[...], 1, 1).astype(BF16)
     attn_ref[...] = attn
-    store(attn_ref, attn_hbm)
     attn = attn.astype(F32)
     prod = attn * saved_ref[...].astype(F32)
     hi = prod.astype(BF16)
     low = (prod - hi.astype(F32)).astype(BF16)
     delta = dot(hi, pick, 1, 0) + dot(low, pick, 1, 0)
     delta_ref[...] = delta.T[:SUB]
+    store(attn_ref, attn_hbm)
     store(delta_ref, delta_hbm)
     picked_g = head_rows(attn.reshape(groups, DIL, D)[:, :SUB])
     delta = jnp.sum(jnp.where(diag, delta.reshape(groups, DIL, 128), 0.0), axis=1)
 
-    for copy in loads[5:]:
-        copy.wait()
     lane = iota((1, 128), 1)
     lse = jnp.concatenate(
         [sum(jnp.where(lane == h, lse_ref[h, :, DIL * j:DIL * (j + 1)], 0.0) for h in range(HEADS))
@@ -128,6 +109,18 @@
     for s in range(seq):
         send_ref[s, :, 0:PROJ] = own[1 if s & MATE else 0]
     store(send_ref.at[:, :, pl.ds(0, PROJ)], send_hbm.at[:, :, pl.ds(0, PROJ)])
+    share = D // seq
+    for i in range(2):
+        wide = slice(HALF * i, HALF * (i + 1))
+        term = dot(saved_ref[:, wide], grad_ref[...], 0, 0)
+        for s in range(seq // 2):
+            here = send_ref.at[i * (seq // 2) + s]
+            here[:, PROJ:PROJ + D] = term[share * s:share * s + 16].astype(BF16)
+            rest = term[share * s + 16:share * s + 24]
+            here[:, PROJ + D:] = jnp.concatenate([rest[:, :D // 2], rest[:, D // 2:]], axis=0).astype(BF16)
+        some = (pl.ds(i * (seq // 2), seq // 2), slice(None), pl.ds(PROJ, TERM))
+        store(send_ref.at[some], send_hbm.at[some])
+
     for copy in stores:
         copy.wait()
 
@@ -147,8 +140,8 @@
         scratch_shapes=[pltpu.VMEM((tok, D), BF16), pltpu.VMEM((tok, D), BF16), pltpu.VMEM((D, D), BF16),
                         pltpu.VMEM((HEADS, 1, tok), F32), pltpu.VMEM((3, tok // DIL, SUB, D), BF16),
                         pltpu.VMEM((tok, D), BF16), pltpu.VMEM((SUB, tok), F32),
-                        pltpu.VMEM((seq, 16, width), BF16), pltpu.VMEM((D, D), F32),
-                        pltpu.SemaphoreType.DMA((9,)), pltpu.SemaphoreType.DMA((5,))],
+                        pltpu.VMEM((seq, 16, width), BF16),
+                        pltpu.SemaphoreType.DMA((7,)), pltpu.SemaphoreType.DMA((5,))],
         compiler_params=pltpu.CompilerParams(vmem_limit_bytes=VMEM),
         cost_estimate=pl.CostEstimate(flops=4 * tok * D * D, bytes_accessed=9 * 10 ** 6, transcendentals=0),
     )(saved, grad, w, lse, view(q), view(k), view(v))
@@ -214,7 +207,7 @@
         + [pl.BlockSpec(memory_space=pl.ANY)] * len(extra),
         out_specs=[col] * 3 + [sums],
         out_shape=[jax.ShapeDtypeStruct((tok, D), BF16)] * 3
-        + [jax.ShapeDtypeStruct((3 * (tok // DIL), D), F32)],
+        + [jax.ShapeDtypeStruct((ROOM, D), F32)],
         input_output_aliases={6 + i: i for i in range(len(before))},
         compiler_params=pltpu.CompilerParams(vmem_limit_bytes=VMEM),
         cost_estimate=pl.CostEstimate(flops=20 * count * tok * tok * HW * 2, bytes_accessed=2 * count * 10 ** 6,
@@ -297,14 +290,11 @@
     )(place, recv, after)
 
 
-def last_kernel(scale, place, mine_ref, theirs_ref, a_ref, b_ref, c_ref, d_ref, sums_hbm,
-                dq_in, dk_in, dv_in, dq_ref, dk_ref, dv_ref, proj_ref, sums_ref, sem):
-    load = pltpu.make_async_copy(sums_hbm, sums_ref, sem)
-    load.start()
+def last_kernel(scale, place, mine_ref, theirs_ref, a_ref, b_ref, c_ref, d_ref, sums_ref,
+                dq_in, dk_in, dv_in, dq_ref, dk_ref, dv_ref, proj_ref):
     proj_ref[...] = ((a_ref[...] + b_ref[...]) + (c_ref[...] + d_ref[...])) * scale
     first = place[0] & MATE == 0
     here = iota((8, SUB, D), 1) == iota((8, SUB, D), 2) // HW
-    load.wait()
     for i, (old, out) in enumerate(((dq_in, dq_ref), (dk_in, dk_ref), (dv_in, dv_ref))):
         part = slice(HALF * i, HALF * (i + 1))
         mine, theirs = mine_ref[:, part], theirs_ref[:, part]
@@ -328,12 +318,11 @@
         grid_spec=pltpu.PrefetchScalarGridSpec(
             num_scalar_prefetch=1,
             grid=(1,),
-            in_specs=[whole(x) for x in small] + [pl.BlockSpec(memory_space=pl.ANY)] + [sub] * 3,
-            out_specs=[sub] * 3 + [whole(terms[0])],
-            scratch_shapes=[pltpu.VMEM(sums.shape, F32), pltpu.SemaphoreType.DMA(())]),
+            in_specs=[whole(x) for x in small] + [pl.BlockSpec((3 * (tok // DIL), D), lambda i, p: (0, 0))] + [sub] * 3,
+            out_specs=[sub] * 3 + [whole(terms[0])]),
         out_shape=[view] * 3 + [jax.ShapeDtypeStruct(terms[0].shape, F32)],
         input_output_aliases={2 + len(small) + i: i for i in range(3)},
-        compiler_params=pltpu.CompilerParams(vmem_limit_bytes=16 * 2 ** 20),
+        compiler_params=pltpu.CompilerParams(vmem_limit_bytes=48 * 2 ** 20),
         cost_estimate=pl.CostEstimate(flops=10 ** 6, bytes_accessed=2 * 10 ** 6, transcendentals=0),
     )(place, *small, sums, *[x.reshape(view.shape) for x in grads])
 

time: 66.9 us -> 64.4 us (0.963)
  Pallas kernels: 49.2 us -> 47.8 us
  local copies, waits for them, and re-layouts: 0.89 us -> 0.01 us
    pallas_call x1, Pallas kernels: 8.51 us -> 7.08 us  [front(): pl.pallas_call(functools.partial(front_kernel, seq), in_specs=[anywhere]...]
    unnamed x6 -> x4, local copies, waits for them, and re-layouts: 0.89 us -> 0.01 us
  transfers between devices with their start and end apart: 5 -> 5, of which waited for: 1 -> 1; matrix products, arithmetic and copies ran while one was open for 0% -> 0% of each run, Pallas kernels for 54% -> 56%
where the time goes in v6:
time: 64.4 us; the launch traced here: 64.1 us
  Pallas kernels  47.8 us (74%)
  starting transfers between devices  15 us (23%)
  between operations  0.7 us (1%)
  waiting for transfers between devices  0.66 us (1%)
    pallas_call x2, Pallas kernels, local_level(): pl.pallas_call(functools.partial(local_kernel, 256, first), grid=(count,)...  35.8 us
    all_to_all x1, starting transfers between devices, on_device(): recv = lax.all_to_all(send, 'seq', 0, 0)  9.54 us
    pallas_call x1, Pallas kernels, front(): pl.pallas_call(functools.partial(front_kernel, seq), in_specs=[anywhere]...  7.08 us
    ppermute x4, starting transfers between devices, other(): return lax.ppermute(x, axis, [(i, i ^ bit) for i in range(size)])  5.47 us
    pallas_call x1, Pallas kernels, dilated_level(): pl.pallas_call(dilated_kernel, grid_spec=pltpu.PrefetchScalarGridSpec(num...  2.71 us
    pallas_call x1, Pallas kernels, last(): pl.pallas_call(functools.partial(last_kernel, scale), grid_spec=pltpu.Pre...  2.11 us
  transfers between devices with their start and end apart: 5, of which 1 were waited for; matrix products, arithmetic and copies ran while one was open for 0% of the time, Pallas kernels for 56%

profile of v6, /device:TPU:2, one launch (start us, length us, event | category | flops | bytes accessed | tf_op | source)
XLA Modules:
  0.0 64.1 jit_solution(5203391533502769650)
XLA Ops:
  0.6 7.1 %shard_map.102 = (bf16[1024,768]{1,0:T(8,128)(2,1)}, f32[16,1024]{1,0:T(8,128)}, bf16[32,16,2048]{2,1,0:T(8,128)(2,1)}) custom-call(bf16[1024,768]{1,0:T(8,128)(2,1)} %bitcast.31, bf16[1024,768]{1,0:T(8,128)(2,1)} %bitcast.32, bf16[768,768]{1,0:T(8,128)(2,1)} %w_hbm.1, f32[12,1,1024]{2,1,0:T(1,128)} %bitcast.33, bf16[8,128,768]{2,1,0:T(8,128)(2,1)} %bitcast.22, ...), custom_call_target="tpu_custom_call" | custom-call | flops 2415919104 | bytes 9000000 | tf_op jit(solution)/shard_map/pallas_call | solution.py:133
  7.7 9.5 %all-to-all-start = ((bf16[32,16,2048]{2,1,0:T(8,128)(2,1)}), bf16[32,16,2048]{2,1,0:T(8,128)(2,1)}, u32[]{:S(2)}, u32[]{:S(2)}) async-start(bf16[32,16,2048]{2,1,0:T(8,128)(2,1)} %get-tuple-element.22), calls=%async_computation | async-start | bytes 4194304 | tf_op jit(solution)/shard_map/all_to_all | solution.py:337
  17.3 28.5 %shard_map.103 = (bf16[1024,768]{1,0:T(8,128)(2,1)}, bf16[1024,768]{1,0:T(8,128)(2,1)}, bf16[1024,768]{1,0:T(8,128)(2,1)}, f32[4096,768]{1,0:T(8,128)}) custom-call(bf16[1024,768]{1,0:T(8,128)(2,1)} %bitcast.23, bf16[1024,768]{1,0:T(8,128)(2,1)} %bitcast.26, bf16[1024,768]{1,0:T(8,128)(2,1)} %bitcast.29, bf16[1024,768]{1,0:T(8,128)(2,1)} %get-tuple-element.23.g_ref, ...), custom_call_target="tpu_custom_call" | custom-call | flops 13421772800 | bytes 10000000 | tf_op jit(solution)/shard_map/pallas_call | solution.py:202
  45.8 0.7 %all-to-all-done.recv_hbm = bf16[32,16,2048]{2,1,0:T(8,128)(2,1)} async-done(((bf16[32,16,2048]{2,1,0:T(8,128)(2,1)}), bf16[32,16,2048]{2,1,0:T(8,128)(2,1)}, u32[]{:S(2)}, u32[]{:S(2)}) %all-to-all-start) | async-done | bytes 2097184 | tf_op jit(solution)/shard_map/all_to_all | solution.py:337
  46.5 2.7 %shard_map.104 = (f32[24,768]{1,0:T(8,128)}, f32[8,1152]{1,0:T(8,128)}, f32[8,1152]{1,0:T(8,128)}) custom-call(s32[1]{0:T(128)} %bitcast.place, bf16[32,16,2048]{2,1,0:T(8,128)(2,1)} %all-to-all-done.recv_hbm, f32[4096,768]{1,0:T(8,128)} %get-tuple-element.25.after.rest_3_), custom_call_target="tpu_custom_call" | custom-call | flops 132120576 | bytes 3000000 | tf_op jit(solution)/shard_map/pallas_call | solution.py:277
  49.2 1.2 %collective-permute-start.3 = (f32[24,768]{1,0:T(8,128)}, f32[24,768]{1,0:T(8,128)S(1)}, u32[]{:S(2)}, u32[]{:S(2)}) collective-permute-start(f32[24,768]{1,0:T(8,128)} %get-tuple-element.28.rest_4_.a_ref), channel_id=1, source_target_pairs={{0,3},{1,2},{2,1},{3,0},{4,7},{5,6},{6,5},{7,4},{8,11},{9,10},{10,... | collective-permute-start | bytes 221192 | tf_op jit(solution)/shard_map/ppermute | solution.py:343
  50.4 1.9 %collective-permute-start.2 = (f32[24,768]{1,0:T(8,128)}, f32[24,768]{1,0:T(8,128)S(1)}, u32[]{:S(2)}, u32[]{:S(2)}) collective-permute-start(f32[24,768]{1,0:T(8,128)} %get-tuple-element.28.rest_4_.a_ref), channel_id=1, source_target_pairs={{0,1},{1,0},{2,3},{3,2},{4,5},{5,4},{6,7},{7,6},{8,9},{9,8},{10,11... | collective-permute-start | bytes 221192 | tf_op jit(solution)/shard_map/ppermute | solution.py:343
  52.3 0.6 collective-permute-start.1
  52.9 1.7 %collective-permute-start = (f32[8,1152]{1,0:T(8,128)}, f32[8,1152]{1,0:T(8,128)S(1)}, u32[]{:S(2)}, u32[]{:S(2)}) collective-permute-start(f32[8,1152]{1,0:T(8,128)} %get-tuple-element.27), channel_id=1, source_target_pairs={{0,16},{4,20},{8,24},{12,28},{16,0},{20,4},{24,8},{28,12},{32,48},... | collective-permute-start | bytes 110600 | tf_op jit(solution)/shard_map/ppermute | solution.py:343
  54.7 0.0 copy-start
  54.7 0.0 copy-start.1
  54.7 7.3 %shard_map.105 = (bf16[1024,768]{1,0:T(8,128)(2,1)}, bf16[1024,768]{1,0:T(8,128)(2,1)}, bf16[1024,768]{1,0:T(8,128)(2,1)}, f32[4096,768]{1,0:T(8,128)}) custom-call(bf16[1024,768]{1,0:T(8,128)(2,1)} %bitcast.24, bf16[1024,768]{1,0:T(8,128)(2,1)} %bitcast.27, ...), custom_call_target="tpu_custom_call", output_to_operand_aliasing={{0}: (6, {}), {1}: (7, {}), {2}: (8, {}), {3}: (9, {})} | custom-call | flops 2684354560 | bytes 2000000 | tf_op jit(solution)/shard_map/pallas_call | solution.py:202
  62.0 0.0 collective-permute-done.theirs_ref
  62.0 0.0 collective-permute-done.3.d_ref
  62.0 0.0 collective-permute-done.2.c_ref
  62.0 0.0 collective-permute-done.1.b_ref
  62.0 0.0 copy-done
  62.0 0.0 copy-done.1
  62.0 2.1 %shard_map.106 = (bf16[8,128,768]{2,1,0:T(8,128)(2,1)}, bf16[8,128,768]{2,1,0:T(8,128)(2,1)}, bf16[8,128,768]{2,1,0:T(8,128)(2,1)}, f32[24,768]{1,0:T(8,128)}) custom-call(s32[1]{0:T(128)} %bitcast.place, f32[8,1152]{1,0:T(8,128)S(1)} %copy-done.1, ...), custom_call_target="tpu_custom_call", output_to_operand_aliasing={{0}: (8, {}), {1}: (9, {}), {2}: (10, {})} | custom-call | flops 1000000 | bytes 2000000 | tf_op jit(solution)/shard_map/pallas_call | solution.py:316
Async XLA Ops:
  7.7 38.7 %all-to-all-start = ((bf16[32,16,2048]{2,1,0:T(8,128)(2,1)}), bf16[32,16,2048]{2,1,0:T(8,128)(2,1)}, u32[]{:S(2)}, u32[]{:S(2)}) async-start(bf16[32,16,2048]{2,1,0:T(8,128)(2,1)} %get-tuple-element.22), calls=%async_computation | async-start | bytes 4194304 | tf_op jit(solution)/shard_map/all_to_all | solution.py:337
  49.2 12.8 %collective-permute-start.3 = (f32[24,768]{1,0:T(8,128)}, f32[24,768]{1,0:T(8,128)S(1)}, u32[]{:S(2)}, u32[]{:S(2)}) collective-permute-start(f32[24,768]{1,0:T(8,128)} %get-tuple-element.28.rest_4_.a_ref), channel_id=1, source_target_pairs={{0,3},{1,2},{2,1},{3,0},{4,7},{5,6},{6,5},{7,4},{8,11},{9,10},{10,... | collective-permute-start | bytes 221192 | tf_op jit(solution)/shard_map/ppermute | solution.py:343
  50.4 11.6 %collective-permute-start.2 = (f32[24,768]{1,0:T(8,128)}, f32[24,768]{1,0:T(8,128)S(1)}, u32[]{:S(2)}, u32[]{:S(2)}) collective-permute-start(f32[24,768]{1,0:T(8,128)} %get-tuple-element.28.rest_4_.a_ref), channel_id=1, source_target_pairs={{0,1},{1,0},{2,3},{3,2},{4,5},{5,4},{6,7},{7,6},{8,9},{9,8},{10,11... | collective-permute-start | bytes 221192 | tf_op jit(solution)/shard_map/ppermute | solution.py:343
  52.3 9.7 %collective-permute-start.1 = (f32[24,768]{1,0:T(8,128)}, f32[24,768]{1,0:T(8,128)S(1)}, u32[]{:S(2)}, u32[]{:S(2)}) collective-permute-start(f32[24,768]{1,0:T(8,128)} %get-tuple-element.28.rest_4_.a_ref), channel_id=1, source_target_pairs={{0,2},{1,3},{2,0},{3,1},{4,6},{5,7},{6,4},{7,5},{8,10},{9,11},{10,... | collective-permute-start | bytes 221192 | tf_op jit(solution)/shard_map/ppermute | solution.py:343
  52.9 9.1 %collective-permute-start = (f32[8,1152]{1,0:T(8,128)}, f32[8,1152]{1,0:T(8,128)S(1)}, u32[]{:S(2)}, u32[]{:S(2)}) collective-permute-start(f32[8,1152]{1,0:T(8,128)} %get-tuple-element.27), channel_id=1, source_target_pairs={{0,16},{4,20},{8,24},{12,28},{16,0},{20,4},{24,8},{28,12},{32,48},... | collective-permute-start | bytes 110600 | tf_op jit(solution)/shard_map/ppermute | solution.py:343
  54.7 7.4 %copy-start = (f32[24,768]{1,0:T(8,128)S(1)}, f32[24,768]{1,0:T(8,128)}, u32[]{:S(2)}) copy-start(f32[24,768]{1,0:T(8,128)} %get-tuple-element.28.rest_4_.a_ref) | copy-start | bytes 221188
  54.7 7.4 %copy-start.1 = (f32[8,1152]{1,0:T(8,128)S(1)}, f32[8,1152]{1,0:T(8,128)}, u32[]{:S(2)}) copy-start(f32[8,1152]{1,0:T(8,128)} %get-tuple-element.26.mine_ref) | copy-start | bytes 110596

commit v7 on v6

--- a/solution.py
+++ b/solution.py
@@ -24,7 +24,7 @@
 TERM = D + D // 2
 MATE = 4
 VMEM = 62 * 2 ** 20
-ROOM = 4096
+ROOM = 8192
 
 
 def dot(a, b, ca, cb):
@@ -169,7 +169,7 @@
         part = slice(c * chunk, (c + 1) * chunk)
         scores = dot(k_stack, q2[part], 1, 1)
         dprobs = dot(v_stack, g2[part], 1, 1)
-        dscores, weights, turned = [], [], []
+        dscores, weights = [], []
         for h in range(2):
             rows = slice(tok * h, tok * (h + 1))
             lse = lse_ref[2 * pair + h, :, part] * LOG2E
@@ -177,11 +177,11 @@
             prob = jnp.exp2(scores[rows] * (SCALE * LOG2E) - lse)
             dscores.append((prob * (dprobs[rows] - delta)).astype(BF16))
             weights.append(prob.astype(BF16))
-            turned.append(dot(k_turned[HW * h:HW * h + HW], dscores[h], 1, 0))
         a = dot(jnp.concatenate(dscores, axis=0), q2[part], 1, 0)
         b = dot(jnp.concatenate(weights, axis=0), g2[part], 1, 0)
         grad_k = a if grad_k is None else grad_k + a
         grad_v = b if grad_v is None else grad_v + b
+        turned = [dot(k_turned[HW * h:HW * h + HW], dscores[h], 1, 0) for h in range(2)]
         grad_q.append(jnp.concatenate(turned, axis=0).T)
     grad_q = jnp.concatenate(grad_q, axis=0) * SCALE
     grad_k = chosen(grad_k) * SCALE
@@ -194,7 +194,7 @@
             jnp.where(keep, val.reshape(groups, DIL, 128), 0.0), axis=1)
 
 
-def local_level(first, count, q, k, v, g, lse, delta, before=(), after=None):
+def local_level(first, count, q, k, v, g, lse, delta, before=(), after=None, limit=56):
     tok = q.shape[0]
     col = pl.BlockSpec((tok, 128), lambda i: (0, first + i))
     sums = pl.BlockSpec((3 * (tok // DIL), 128), lambda i: (0, first + i))
@@ -209,7 +209,7 @@
         out_shape=[jax.ShapeDtypeStruct((tok, D), BF16)] * 3
         + [jax.ShapeDtypeStruct((ROOM, D), F32)],
         input_output_aliases={6 + i: i for i in range(len(before))},
-        compiler_params=pltpu.CompilerParams(vmem_limit_bytes=VMEM),
+        compiler_params=pltpu.CompilerParams(vmem_limit_bytes=limit * 2 ** 20),
         cost_estimate=pl.CostEstimate(flops=20 * count * tok * tok * HW * 2, bytes_accessed=2 * count * 10 ** 6,
                                       transcendentals=2 * count * tok * tok),
     )(q, k, v, g, lse, delta, *extra)
@@ -284,7 +284,7 @@
             scratch_shapes=[pltpu.VMEM((seq, 16, PROJ), BF16), pltpu.VMEM((seq, 16, TERM), BF16),
                             pltpu.SemaphoreType.DMA((2,))]),
         out_shape=[jax.ShapeDtypeStruct((24, D), F32)] + [jax.ShapeDtypeStruct((8, 3 * HALF), F32)] * 2,
-        compiler_params=pltpu.CompilerParams(vmem_limit_bytes=VMEM),
+        compiler_params=pltpu.CompilerParams(vmem_limit_bytes=40 * 2 ** 20),
         cost_estimate=pl.CostEstimate(flops=7 * 2 * 96 * 256 * HALF, bytes_accessed=3 * 10 ** 6,
                                       transcendentals=2 * 96 * 256),
     )(place, recv, after)
@@ -344,7 +344,7 @@
 
     theirs = other(theirs, "seq", seq, MATE)
     terms = (term, *[other(term, "rep", rep, bit) for bit in (2, 1, 3)])
-    part = local_level(5, 1, q, k, v, attn, lse, delta, before=part, after=term)
+    part = local_level(5, 1, q, k, v, attn, lse, delta, before=part, after=term, limit=40)
     *outs, projection_gradient = last(me, mine, theirs, part[3], terms, part[:3], 1.0 / math.sqrt(rep * seq * tok))
     return (*[x.reshape(1, tok, D) for x in outs], projection_gradient)
 

time: 64.4 us -> 61.4 us (0.953)
  Pallas kernels: 47.8 us -> 44.5 us
    pallas_call x2, Pallas kernels: 35.8 us -> 34.1 us  [local_level(): pl.pallas_call(functools.partial(local_kernel, 256, first), grid=(count,)...]
    pallas_call x1, Pallas kernels: 2.71 us -> 1.2 us  [dilated_level(): pl.pallas_call(dilated_kernel, grid_spec=pltpu.PrefetchScalarGridSpec(num...]
where the time goes in v7:
time: 61.4 us; the launch traced here: 61.2 us
  Pallas kernels  44.5 us (72%)
  starting transfers between devices  15 us (24%)
  waiting for transfers between devices  0.97 us (2%)
  between operations  0.73 us (1%)
    pallas_call x2, Pallas kernels, local_level(): pl.pallas_call(functools.partial(local_kernel, 256, first), grid=(count,)...  34.1 us
    all_to_all x1, starting transfers between devices, on_device(): recv = lax.all_to_all(send, 'seq', 0, 0)  9.49 us
    pallas_call x1, Pallas kernels, front(): pl.pallas_call(functools.partial(front_kernel, seq), in_specs=[anywhere]...  7.07 us
    ppermute x4, starting transfers between devices, other(): return lax.ppermute(x, axis, [(i, i ^ bit) for i in range(size)])  5.47 us
    pallas_call x1, Pallas kernels, last(): pl.pallas_call(functools.partial(last_kernel, scale), grid_spec=pltpu.Pre...  2.11 us
  transfers between devices with their start and end apart: 5, of which 1 were waited for; matrix products, arithmetic and copies ran while one was open for 0% of the time, Pallas kernels for 56%

profile of v7, /device:TPU:2, one launch (start us, length us, event | category | flops | bytes accessed | tf_op | source)
XLA Modules:
  0.0 61.2 jit_solution(85299547673875676)
XLA Ops:
  0.6 7.1 %shard_map.102 = (bf16[1024,768]{1,0:T(8,128)(2,1)}, f32[16,1024]{1,0:T(8,128)}, bf16[32,16,2048]{2,1,0:T(8,128)(2,1)}) custom-call(bf16[1024,768]{1,0:T(8,128)(2,1)} %bitcast.34, bf16[1024,768]{1,0:T(8,128)(2,1)} %bitcast.35, bf16[768,768]{1,0:T(8,128)(2,1)} %w_hbm.1, f32[12,1,1024]{2,1,0:T(1,128)} %bitcast.25, bf16[8,128,768]{2,1,0:T(8,128)(2,1)} %bitcast.16, ...), custom_call_target="tpu_custom_call" | custom-call | flops 2415919104 | bytes 9000000 | tf_op jit(solution)/shard_map/pallas_call | solution.py:133
  7.7 9.5 %all-to-all-start = ((bf16[32,16,2048]{2,1,0:T(8,128)(2,1)}), bf16[32,16,2048]{2,1,0:T(8,128)(2,1)S(1)}, u32[]{:S(2)}, u32[]{:S(2)}) async-start(bf16[32,16,2048]{2,1,0:T(8,128)(2,1)} %get-tuple-element.22), calls=%async_computation | async-start | bytes 4194304 | tf_op jit(solution)/shard_map/all_to_all | solution.py:337
  17.2 28.2 %shard_map.103 = (bf16[1024,768]{1,0:T(8,128)(2,1)}, bf16[1024,768]{1,0:T(8,128)(2,1)}, bf16[1024,768]{1,0:T(8,128)(2,1)}, f32[8192,768]{1,0:T(8,128)}) custom-call(bf16[1024,768]{1,0:T(8,128)(2,1)} %bitcast.17, bf16[1024,768]{1,0:T(8,128)(2,1)} %bitcast.20, bf16[1024,768]{1,0:T(8,128)(2,1)} %bitcast.23, bf16[1024,768]{1,0:T(8,128)(2,1)} %get-tuple-element.23.g_ref, ...), custom_call_target="tpu_custom_call" | custom-call | flops 13421772800 | bytes 10000000 | tf_op jit(solution)/shard_map/pallas_call | solution.py:202
  45.4 1.0 %all-to-all-done.recv_hbm = bf16[32,16,2048]{2,1,0:T(8,128)(2,1)S(1)} async-done(((bf16[32,16,2048]{2,1,0:T(8,128)(2,1)}), bf16[32,16,2048]{2,1,0:T(8,128)(2,1)S(1)}, u32[]{:S(2)}, u32[]{:S(2)}) %all-to-all-start) | async-done | bytes 2097184 | tf_op jit(solution)/shard_map/all_to_all | solution.py:337
  46.3 0.0 copy-start
  46.4 0.0 copy-start.4
  46.4 0.0 copy-start.5
  46.4 1.2 %shard_map.104 = (f32[24,768]{1,0:T(8,128)S(1)}, f32[8,1152]{1,0:T(8,128)S(1)}, f32[8,1152]{1,0:T(8,128)S(1)}) custom-call(s32[1]{0:T(128)} %bitcast.place, bf16[32,16,2048]{2,1,0:T(8,128)(2,1)S(1)} %all-to-all-done.recv_hbm, f32[8192,768]{1,0:T(8,128)} %get-tuple-element.25.after.rest_3_), custom_call_target="tpu_custom_call" | custom-call | flops 132120576 | bytes 3000000 | tf_op jit(solution)/shard_map/pallas_call | solution.py:277
  47.6 0.9 %collective-permute-start.3 = (f32[24,768]{1,0:T(8,128)S(1)}, f32[24,768]{1,0:T(8,128)S(1)}, u32[]{:S(2)}, u32[]{:S(2)}) collective-permute-start(f32[24,768]{1,0:T(8,128)S(1)} %get-tuple-element.28.rest_4_.a_ref), channel_id=1, source_target_pairs={{0,3},{1,2},{2,1},{3,0},{4,7},{5,6},{6,5},{7,4},{8,11},{9,10},{10,... | collective-permute-start | bytes 221192 | tf_op jit(solution)/shard_map/ppermute | solution.py:343
  48.5 2.1 %collective-permute-start.2 = (f32[24,768]{1,0:T(8,128)S(1)}, f32[24,768]{1,0:T(8,128)S(1)}, u32[]{:S(2)}, u32[]{:S(2)}) collective-permute-start(f32[24,768]{1,0:T(8,128)S(1)} %get-tuple-element.28.rest_4_.a_ref), channel_id=1, source_target_pairs={{0,1},{1,0},{2,3},{3,2},{4,5},{5,4},{6,7},{7,6},{8,9},{9,8},{10,11... | collective-permute-start | bytes 221192 | tf_op jit(solution)/shard_map/ppermute | solution.py:343
  50.7 0.6 %collective-permute-start.1 = (f32[24,768]{1,0:T(8,128)S(1)}, f32[24,768]{1,0:T(8,128)S(1)}, u32[]{:S(2)}, u32[]{:S(2)}) collective-permute-start(f32[24,768]{1,0:T(8,128)S(1)} %get-tuple-element.28.rest_4_.a_ref), channel_id=1, source_target_pairs={{0,2},{1,3},{2,0},{3,1},{4,6},{5,7},{6,4},{7,5},{8,10},{9,11},{10,... | collective-permute-start | bytes 221192 | tf_op jit(solution)/shard_map/ppermute | solution.py:343
  51.3 1.7 %collective-permute-start = (f32[8,1152]{1,0:T(8,128)S(1)}, f32[8,1152]{1,0:T(8,128)S(1)}, u32[]{:S(2)}, u32[]{:S(2)}) collective-permute-start(f32[8,1152]{1,0:T(8,128)S(1)} %get-tuple-element.27), channel_id=1, source_target_pairs={{0,16},{4,20},{8,24},{12,28},{16,0},{20,4},{24,8},{28,12},{32,48},... | collective-permute-start | bytes 110600 | tf_op jit(solution)/shard_map/ppermute | solution.py:343
  53.1 0.0 copy-done
  53.1 0.0 copy-done.1
  53.1 0.0 copy-done.2
  53.1 0.0 copy-done.3
  53.1 0.0 copy-done.4
  53.1 0.0 copy-done.5
  53.1 5.9 %shard_map.105 = (bf16[1024,768]{1,0:T(8,128)(2,1)}, bf16[1024,768]{1,0:T(8,128)(2,1)}, bf16[1024,768]{1,0:T(8,128)(2,1)}, f32[8192,768]{1,0:T(8,128)}) custom-call(bf16[1024,768]{1,0:T(8,128)(2,1)S(1)} %bitcast.18, bf16[1024,768]{1,0:T(8,128)(2,1)S(1)} %bitcast.21, ...), custom_call_target="tpu_custom_call", output_to_operand_aliasing={{0}: (6, {}), {1}: (7, {}), {2}: (8, {}), {3}: (9, {})} | custom-call | flops 2684354560 | bytes 2000000 | tf_op jit(solution)/shard_map/pallas_call | solution.py:202
  59.0 0.0 collective-permute-done.theirs_ref
  59.0 0.0 collective-permute-done.3.d_ref
  59.0 0.0 collective-permute-done.2.c_ref
  59.1 0.0 collective-permute-done.1.b_ref
  59.1 2.1 %shard_map.106 = (bf16[8,128,768]{2,1,0:T(8,128)(2,1)}, bf16[8,128,768]{2,1,0:T(8,128)(2,1)}, bf16[8,128,768]{2,1,0:T(8,128)(2,1)}, f32[24,768]{1,0:T(8,128)}) custom-call(s32[1]{0:T(128)} %bitcast.place, f32[8,1152]{1,0:T(8,128)S(1)} %get-tuple-element.26.mine_ref, ...), custom_call_target="tpu_custom_call", output_to_operand_aliasing={{0}: (8, {}), {1}: (9, {}), {2}: (10, {})} | custom-call | flops 1000000 | bytes 2000000 | tf_op jit(solution)/shard_map/pallas_call | solution.py:316
  (3 shorter events, 0.0 us)
Async XLA Ops:
  7.7 38.6 %all-to-all-start = ((bf16[32,16,2048]{2,1,0:T(8,128)(2,1)}), bf16[32,16,2048]{2,1,0:T(8,128)(2,1)S(1)}, u32[]{:S(2)}, u32[]{:S(2)}) async-start(bf16[32,16,2048]{2,1,0:T(8,128)(2,1)} %get-tuple-element.22), calls=%async_computation | async-start | bytes 4194304 | tf_op jit(solution)/shard_map/all_to_all | solution.py:337
  46.3 6.7 %copy-start = (bf16[1,1024,768]{2,1,0:T(8,128)(2,1)S(1)}, bf16[1,1024,768]{2,1,0:T(8,128)(2,1)}, u32[]{:S(2)}) copy-start(bf16[1,1024,768]{2,1,0:T(8,128)(2,1)} %param.7) | copy-start | bytes 4718596
  46.3 6.7 %copy-start.1 = (bf16[1,1024,768]{2,1,0:T(8,128)(2,1)S(1)}, bf16[1,1024,768]{2,1,0:T(8,128)(2,1)}, u32[]{:S(2)}) copy-start(bf16[1,1024,768]{2,1,0:T(8,128)(2,1)} %param.8) | copy-start | bytes 4718596
  46.3 6.7 %copy-start.2 = (bf16[1,1024,768]{2,1,0:T(8,128)(2,1)S(1)}, bf16[1,1024,768]{2,1,0:T(8,128)(2,1)}, u32[]{:S(2)}) copy-start(bf16[1,1024,768]{2,1,0:T(8,128)(2,1)} %param.9) | copy-start | bytes 4718596
  46.3 6.7 %copy-start.3 = (bf16[1024,768]{1,0:T(8,128)(2,1)S(1)}, bf16[1024,768]{1,0:T(8,128)(2,1)}, u32[]{:S(2)}) copy-start(bf16[1024,768]{1,0:T(8,128)(2,1)} %get-tuple-element.23.g_ref) | copy-start | bytes 4718596
  46.4 6.7 %copy-start.4 = (f32[1,12,1024]{2,0,1:T(1,128)S(1)}, f32[1,12,1024]{2,0,1:T(1,128)}, u32[]{:S(2)}) copy-start(f32[1,12,1024]{2,0,1:T(1,128)} %param.11) | copy-start | bytes 147460
  46.4 6.7 %copy-start.5 = (f32[16,1024]{1,0:T(8,128)S(1)}, f32[16,1024]{1,0:T(8,128)}, u32[]{:S(2)}) copy-start(f32[16,1024]{1,0:T(8,128)} %get-tuple-element.24.delta_ref) | copy-start | bytes 196612
  47.6 11.5 %collective-permute-start.3 = (f32[24,768]{1,0:T(8,128)S(1)}, f32[24,768]{1,0:T(8,128)S(1)}, u32[]{:S(2)}, u32[]{:S(2)}) collective-permute-start(f32[24,768]{1,0:T(8,128)S(1)} %get-tuple-element.28.rest_4_.a_ref), channel_id=1, source_target_pairs={{0,3},{1,2},{2,1},{3,0},{4,7},{5,6},{6,5},{7,4},{8,11},{9,10},{10,... | collective-permute-start | bytes 221192 | tf_op jit(solution)/shard_map/ppermute | solution.py:343
  48.5 10.5 %collective-permute-start.2 = (f32[24,768]{1,0:T(8,128)S(1)}, f32[24,768]{1,0:T(8,128)S(1)}, u32[]{:S(2)}, u32[]{:S(2)}) collective-permute-start(f32[24,768]{1,0:T(8,128)S(1)} %get-tuple-element.28.rest_4_.a_ref), channel_id=1, source_target_pairs={{0,1},{1,0},{2,3},{3,2},{4,5},{5,4},{6,7},{7,6},{8,9},{9,8},{10,11... | collective-permute-start | bytes 221192 | tf_op jit(solution)/shard_map/ppermute | solution.py:343
  50.7 8.4 %collective-permute-start.1 = (f32[24,768]{1,0:T(8,128)S(1)}, f32[24,768]{1,0:T(8,128)S(1)}, u32[]{:S(2)}, u32[]{:S(2)}) collective-permute-start(f32[24,768]{1,0:T(8,128)S(1)} %get-tuple-element.28.rest_4_.a_ref), channel_id=1, source_target_pairs={{0,2},{1,3},{2,0},{3,1},{4,6},{5,7},{6,4},{7,5},{8,10},{9,11},{10,... | collective-permute-start | bytes 221192 | tf_op jit(solution)/shard_map/ppermute | solution.py:343
  51.3 7.7 %collective-permute-start = (f32[8,1152]{1,0:T(8,128)S(1)}, f32[8,1152]{1,0:T(8,128)S(1)}, u32[]{:S(2)}, u32[]{:S(2)}) collective-permute-start(f32[8,1152]{1,0:T(8,128)S(1)} %get-tuple-element.27), channel_id=1, source_target_pairs={{0,16},{4,20},{8,24},{12,28},{16,0},{20,4},{24,8},{28,12},{32,48},... | collective-permute-start | bytes 110600 | tf_op jit(solution)/shard_map/ppermute | solution.py:343
